TPU v7x, 32 devices: a whole 2x2x4 slice. The times are simulated.
32 devices in a mesh: dp: 4 (over y, core), expert: 8 (over z, x).
Axes of the slice: x: 2, y: 2, z: 4, core: 2. Of those that a mesh axis runs over, the one named last changes fastest.
Arguments:
- tokens: bfloat16 [384, 3584], P('dp', 'expert'), may hold values from -13 to 13
- routes: int32 [384, 8], replicated, may hold values from 0 to 31, all different within a row; in each aligned block of 96 rows (0 to 95, 96 to 191, ...) at most 32 rows name the same one
- gate_weight: bfloat16 [32, 3584, 2048], P('expert', None, 'dp'), may hold values from -0.09375 to 0.09375
- up_weight: bfloat16 [32, 3584, 2048], P('expert', None, 'dp'), may hold values from -0.09375 to 0.09375
- hidden_grad: bfloat16 [32, 4, 32, 2048], P('expert', None, None, 'dp'), may hold values from -40 to 40
- clip_limit: float32 [32], P('expert'), may hold values from 1 to 40
Outputs:
- hidden: bfloat16 [32, 4, 32, 2048], P('expert', None, None, 'dp')
- grad_gate: bfloat16 [32, 3584, 2048], P('expert', None, 'dp')
- grad_up: bfloat16 [32, 3584, 2048], P('expert', None, 'dp')
- token_grad: bfloat16 [384, 3584], P('dp', 'expert')
Inputs may be any that keep to these rules, and one draw needn't show every extreme that they name: `routes`: each row names 8 different experts. In each aligned block of 96 rows (the tokens of one index of dp) no expert is named by more than 32 rows, a bound that some block reaches.
All inputs are finite; a program needn't handle non-finite values.
Results may differ from a plain program's by a relative error of at most 0.014.
Values may be sent and summed in bfloat16 or wider, within the bound.
A program may use at most 192 MiB of HBM per device.

v0:
```python
import jax
import jax.numpy as jnp
from jax import lax
from jax.sharding import PartitionSpec as P


def slot_tables(block_routes, experts, capacity, top_count):
    flat_routes = block_routes.reshape(-1)
    expert_ids = jnp.arange(experts, dtype=jnp.int32)
    onehot = (flat_routes[:, None] == expert_ids[None, :]).astype(jnp.int32)
    before = jnp.cumsum(onehot, axis=0) - onehot
    slot_ranks = jnp.sum(before * onehot, axis=1)
    owner_token = jnp.arange(flat_routes.shape[0], dtype=jnp.int32) // top_count
    token_of = (
        jnp.zeros((experts, capacity), jnp.int32).at[flat_routes, slot_ranks].set(owner_token)
    )
    occupied = jnp.zeros((experts, capacity), jnp.bool_).at[flat_routes, slot_ranks].set(True)
    return (slot_ranks.reshape(block_routes.shape), token_of, occupied)


def expert_math(row_block, grad_block, gate_w, up_w):
    gate_pre = jnp.dot(row_block, gate_w, preferred_element_type=jnp.float32)
    up_pre = jnp.dot(row_block, up_w, preferred_element_type=jnp.float32)
    sigma_gate = jax.nn.sigmoid(gate_pre)
    hidden_rows = (gate_pre * sigma_gate * up_pre).astype(jnp.bfloat16)
    grad_float = grad_block.astype(jnp.float32)
    up_act = (grad_float * gate_pre * sigma_gate).astype(jnp.bfloat16)
    gate_act = (grad_float * up_pre * sigma_gate * (1.0 + gate_pre * (1.0 - sigma_gate))).astype(
        jnp.bfloat16
    )
    over_rows = (((0,), (0,)), ((), ()))
    over_units = (((1,), (1,)), ((), ()))
    raw_gate = lax.dot_general(row_block, gate_act, over_rows, preferred_element_type=jnp.float32)
    raw_up = lax.dot_general(row_block, up_act, over_rows, preferred_element_type=jnp.float32)
    partial_value = lax.dot_general(
        gate_act, gate_w, over_units, preferred_element_type=jnp.float32
    )
    partial_value = partial_value + lax.dot_general(
        up_act, up_w, over_units, preferred_element_type=jnp.float32
    )
    return (hidden_rows, raw_gate, raw_up, partial_value)


def body(tokens, routes, gate_weight, up_weight, hidden_grad, clip_limit):
    dp_count = lax.axis_size("dp")
    expert_count = lax.axis_size("expert")
    local_experts = gate_weight.shape[0]
    experts = local_experts * expert_count
    capacity = hidden_grad.shape[2]
    hidden_units = gate_weight.shape[2]
    model_width = gate_weight.shape[1]
    top_count = routes.shape[1]
    tok_rows = tokens.shape[0]
    dp_index = lax.axis_index("dp")
    blocks = routes.reshape(dp_count, tok_rows, top_count)
    own_routes = lax.dynamic_index_in_dim(blocks, dp_index, 0, keepdims=False)
    slot_ranks, token_of, occupied = slot_tables(own_routes, experts, capacity, top_count)
    outgoing = jnp.where(occupied[:, :, None], tokens[token_of], jnp.zeros((), tokens.dtype))[
        :, None
    ]
    arrived = lax.all_to_all(outgoing, "expert", split_axis=0, concat_axis=3, tiled=True)
    gathered = lax.all_gather(arrived, "dp", axis=1, tiled=True)
    hidden_list = []
    gate_list = []
    up_list = []
    partial_list = []
    squares = []
    for expert_item in range(local_experts):
        row_block = gathered[expert_item].reshape(dp_count * capacity, model_width)
        grad_block = hidden_grad[expert_item].reshape(dp_count * capacity, hidden_units)
        hidden_rows, raw_gate, raw_up, partial_value = expert_math(
            row_block, grad_block, gate_weight[expert_item], up_weight[expert_item]
        )
        hidden_list.append(hidden_rows.reshape(dp_count, capacity, hidden_units))
        gate_list.append(raw_gate)
        up_list.append(raw_up)
        partial_list.append(partial_value.reshape(dp_count, capacity, model_width))
        squares.append(jnp.sum(raw_gate * raw_gate) + jnp.sum(raw_up * raw_up))
    totals = lax.psum(jnp.stack(squares), "dp")
    root_mean = jnp.sqrt(totals / (2.0 * model_width * hidden_units * dp_count) + 1e-06)
    clip_scale = jnp.minimum(1.0, clip_limit / root_mean)
    grad_gate = (clip_scale[:, None, None] * jnp.stack(gate_list)).astype(jnp.bfloat16)
    grad_up = (clip_scale[:, None, None] * jnp.stack(up_list)).astype(jnp.bfloat16)
    hidden = jnp.stack(hidden_list)
    partials = jnp.stack(partial_list)
    own_sums = lax.psum_scatter(
        partials.astype(jnp.bfloat16), "dp", scatter_dimension=1, tiled=True
    ).astype(jnp.float32)
    returned = lax.all_to_all(
        own_sums.astype(jnp.bfloat16), "expert", split_axis=3, concat_axis=0, tiled=True
    ).astype(own_sums.dtype)
    flat_back = returned.reshape(experts * capacity, -1)
    picked = flat_back[own_routes * capacity + slot_ranks]
    token_grad = jnp.sum(picked, axis=1).astype(jnp.bfloat16)
    return (hidden, grad_gate, grad_up, token_grad)


def solution(mesh):
    placed = (
        P("dp", "expert"),
        P(),
        P("expert", None, "dp"),
        P("expert", None, "dp"),
        P("expert", None, None, "dp"),
        P("expert"),
    )
    return jax.shard_map(
        body,
        mesh=mesh,
        in_specs=placed,
        out_specs=(
            P("expert", None, None, "dp"),
            P("expert", None, "dp"),
            P("expert", None, "dp"),
            P("dp", "expert"),
        ),
        check_vma=False,
    )
```

profile of v0, /device:TPU:0, one launch (start us, length us, event | category | flops | bytes accessed | tf_op | source)
XLA Modules:
  0.0 355.8 jit_solution(12962711743785473100)
XLA Ops:
  7.2 0.8 copy.24
  8.4 1.7 reduce-window.6
  10.6 37.4 %scatter_fusion.1 = s32[32,32]{1,0:T(8,128)S(1)} fusion(s32[32,32]{1,0:T(8,128)S(1)} %broadcast.116, s32[768]{0:T(1024)S(1)} %fusion.78, s32[768]{0:T(1024)S(1)} %add_select_fusion), kind=kCustom, calls=%fused_computation.3 | custom fusion | bytes 15360 | tf_op jit(solution)/shard_map/scatter | solution.py:15
  48.1 38.1 %scatter_fusion = pred[32,32]{1,0:T(8,128)(4,1)S(1)} fusion(pred[32,32]{1,0:T(8,128)(4,1)S(1)} %broadcast_in_dim.18, s32[768]{0:T(1024)S(1)} %fusion.78, pred[768]{0:T(1024)(128)(4,1)S(1)} %broadcast.154), kind=kCustom, calls=%fused_computation.2 | custom fusion | bytes 8448 | tf_op jit(solution)/shard_map/scatter | solution.py:17
  86.2 4.0 %gather_fusion = bf16[1024,448]{1,0:T(8,128)(2,1)S(1)} fusion(bf16[96,448]{1,0:T(8,128)(2,1)S(1)} %copy-done, s32[1024]{0:T(1024)S(1)} %broadcast_clamp_fusion), kind=kCustom, calls=%fused_computation | custom fusion | bytes 1839104 | tf_op jit(solution)/shard_map/gather | solution.py:58
  90.4 32.8 %all_to_all.27 = bf16[32,1,32,448]{3,2,1,0:T(8,128)(2,1)S(1)} all-to-all(bf16[32,1,32,448]{3,2,1,0:T(8,128)(2,1)S(1)} %broadcast_select_fusion), channel_id=1, replica_groups=mesh['dp'=4,'expert'=8] {'expert'}, dimensions={0} | all-to-all | bytes 1835008 | tf_op jit(solution)/shard_map/all_to_all | solution.py:61
  123.3 0.6 copy.27
  123.8 2.1 all_to_all.23
  126.5 30.2 %all-gather.2.cloned.1.call-done = bf16[4,4,32,3584]{3,2,0,1:T(8,128)(2,1)} async-done(((bf16[4,1,32,3584]{3,2,0,1:T(8,128)(2,1)}), bf16[4,4,32,3584]{3,2,0,1:T(8,128)(2,1)}) %all-gather.2.cloned.1.call-update) | async-done | bytes 3670032 | tf_op jit(solution)/shard_map/all_gather | solution.py:62
  156.6 2.3 fusion.79
  159.0 2.8 fusion.11
  161.8 2.9 fusion.67
  164.7 3.9 %fusion.9 = f32[128,3584]{1,0:T(8,128)S(1)} fusion(bf16[128,512]{1,0:T(8,128)(2,1)S(1)} %get-tuple-element.18, bf16[4,3584,512]{2,1,0:T(8,128)(2,1)} %param.8), kind=kOutput, calls=%fused_computation.28 | convolution fusion | flops 469762048 | bytes 5636096 | tf_op jit(solution)/shard_map/dot_general | solution.py:35
  168.7 5.5 %multiply_reduce_fusion.1 = (f32[]{:T(128)}, f32[3584,512]{1,0:T(8,128)}) fusion(bf16[128,3584]{1,0:T(8,128)(2,1)S(1)} %bitcast.194, bf16[128,512]{1,0:T(8,128)(2,1)S(1)} %get-tuple-element.18), kind=kOutput, calls=%fused_computation.9 | convolution fusion | flops 473432064 | bytes 8388612 | tf_op jit(solution)/shard_map/dot_general | solution.py:33
  174.2 2.8 fusion.32
  177.0 0.7 fusion.52
  177.8 1.3 fusion.30
  179.1 4.8 %multiply_reduce_fusion.7 = (f32[]{:T(128)}, f32[3584,512]{1,0:T(8,128)}) fusion(bf16[128,3584]{1,0:T(8,128)(2,1)S(1)} %bitcast.198, bf16[128,512]{1,0:T(8,128)(2,1)S(1)} %get-tuple-element.8), kind=kOutput, calls=%fused_computation.15 | convolution fusion | flops 473432064 | bytes 8388612 | tf_op jit(solution)/shard_map/dot_general | solution.py:33
  183.9 0.6 fusion.18
  184.5 0.6 fusion.25
  185.2 0.7 fusion.57
  185.9 2.5 fusion.23
  188.4 0.7 fusion.62
  189.1 2.5 fusion.16
  191.6 4.7 %multiply_reduce_fusion.6 = (f32[]{:T(128)}, f32[3584,512]{1,0:T(8,128)}) fusion(bf16[128,3584]{1,0:T(8,128)(2,1)S(1)} %bitcast.199, bf16[128,512]{1,0:T(8,128)(2,1)S(1)} %get-tuple-element.20), kind=kOutput, calls=%fused_computation.14 | convolution fusion | flops 473432064 | bytes 8388612 | tf_op jit(solution)/shard_map/dot_general | solution.py:34
  196.4 1.5 fusion.2
  197.9 4.7 %multiply_reduce_fusion = (f32[]{:T(128)}, f32[3584,512]{1,0:T(8,128)}) fusion(bf16[128,3584]{1,0:T(8,128)(2,1)S(1)} %bitcast.195, bf16[128,512]{1,0:T(8,128)(2,1)S(1)} %get-tuple-element.23), kind=kOutput, calls=%fused_computation.8 | convolution fusion | flops 473432064 | bytes 8388612 | tf_op jit(solution)/shard_map/dot_general | solution.py:34
  202.6 1.3 fusion.5
  203.9 1.3 fusion.3
  205.3 1.3 fusion.4
  206.6 2.1 pad_maximum_fusion
  208.7 4.7 %multiply_reduce_fusion.2 = (f32[]{:T(128)}, f32[3584,512]{1,0:T(8,128)}) fusion(bf16[128,3584]{1,0:T(8,128)(2,1)S(1)} %bitcast.190, bf16[128,512]{1,0:T(8,128)(2,1)S(1)} %get-tuple-element.22), kind=kOutput, calls=%fused_computation.10 | convolution fusion | flops 473432064 | bytes 8388612 | tf_op jit(solution)/shard_map/dot_general | solution.py:34
  215.9 4.7 %multiply_reduce_fusion.3 = (f32[]{:T(128)}, f32[3584,512]{1,0:T(8,128)}) fusion(bf16[128,3584]{1,0:T(8,128)(2,1)S(1)} %bitcast.191, bf16[128,512]{1,0:T(8,128)(2,1)S(1)} %get-tuple-element.16), kind=kOutput, calls=%fused_computation.11 | convolution fusion | flops 473432064 | bytes 8388612 | tf_op jit(solution)/shard_map/dot_general | solution.py:33
  221.9 4.7 %multiply_reduce_fusion.4 = (f32[]{:T(128)}, f32[3584,512]{1,0:T(8,128)}) fusion(bf16[128,3584]{1,0:T(8,128)(2,1)S(1)} %bitcast.186, bf16[128,512]{1,0:T(8,128)(2,1)S(1)} %get-tuple-element.21), kind=kOutput, calls=%fused_computation.12 | convolution fusion | flops 473432064 | bytes 8388612 | tf_op jit(solution)/shard_map/dot_general | solution.py:34
  226.7 4.7 %multiply_reduce_fusion.5 = (f32[]{:T(128)}, f32[3584,512]{1,0:T(8,128)}) fusion(bf16[128,3584]{1,0:T(8,128)(2,1)S(1)} %bitcast.187, bf16[128,512]{1,0:T(8,128)(2,1)S(1)} %get-tuple-element.14), kind=kOutput, calls=%fused_computation.13 | convolution fusion | flops 473432064 | bytes 8388612 | tf_op jit(solution)/shard_map/dot_general | solution.py:33
  232.8 0.6 dynamic-slice
  233.4 7.0 %psum.7 = f32[4]{0:T(128)S(1)} all-reduce(f32[4]{0:T(128)S(1)} %pad_maximum_fusion.2), channel_id=1, replica_groups=mesh['dp'=4,'expert'=8] {'dp'}, use_global_device_ids=true, to_apply=%region_13.14 | all-reduce | flops 4 | bytes 32 | tf_op jit(solution)/shard_map/psum | solution.py:79
  240.5 45.5 %all-reduce.3.cloned.1.call-done = bf16[4,4,32,3584]{3,2,1,0:T(8,128)(2,1)} async-done(((bf16[4,4,32,3584]{3,2,1,0:T(8,128)(2,1)}), bf16[4,4,32,3584]{3,2,1,0:T(8,128)(2,1)}) %all-reduce.3.cloned.1.call-update) | async-done | bytes 3670032
  286.0 1.9 constant_dynamic-slice_fusion
  287.9 3.9 %copy.28 = bf16[4,1,32,3584]{2,0,1,3:T(4,128)(2,1)} copy(bf16[4,1,32,3584]{3,2,1,0:T(8,128)(2,1)S(1)} %constant_dynamic-slice_fusion) | data formatting | bytes 1835008 | tf_op jit(solution)/shard_map/reduce_scatter | solution.py:86
  291.7 5.8 %reshape.181 = bf16[8,2,28672]{2,1,0:T(2,128)(2,1)} reshape(bf16[3584,1,4,32]{3,2,1,0:T(4,128)(2,1)} %bitcast.204) | data formatting | bytes 1835008
  297.5 5.5 %all-to-all-start.1 = ((bf16[8,2,28672]{2,1,0:T(2,128)(2,1)}), bf16[8,2,28672]{2,1,0:T(2,128)(2,1)S(1)}, u32[]{:S(2)}, u32[]{:S(2)}) async-start(bf16[8,2,28672]{2,1,0:T(2,128)(2,1)} %reshape.181), calls=%async_computation.1 | async-start | bytes 1835008 | tf_op jit(solution)/shard_map/all_to_all | solution.py:89
  303.0 30.4 %fusion.1 = (bf16[4,3584,512]{2,1,0:T(8,128)(2,1)}, bf16[4,3584,512]{2,1,0:T(8,128)(2,1)}) fusion(f32[1,3584,512]{2,1,0:T(8,128)} %bitcast.179, f32[1,3584,512]{2,1,0:T(8,128)} %bitcast.180, f32[1,3584,512]{2,1,0:T(8,128)} %bitcast.182, f32[1,3584,512]{2,1,0:T(8,128)} %bitcast.178, f32[4]{0:T(128)S(1)} %multiply_minimum_fusion, f32[1,3584,512]{2,1,0:T(8,128)} %bitcast.176, ...), kind=kLoop, calls=%fused_computation.7 | loop fusion | flops 73400320 | bytes 88080400 | tf_op jit(solution)/shard_map/convert_element_type | solution.py:83
  333.4 0.9 pad_maximum_fusion.1
  334.3 3.3 reshape.182
  337.5 5.9 %copy.29 = f32[4,1,32,8,448]{4,2,0,3,1:T(8,128)S(1)} copy(bf16[4,1,32,8,448]{2,0,4,3,1:T(4,128)(2,1)} %bitcast.205) | data formatting | bytes 2752512 | tf_op jit(solution)/shard_map/convert_element_type | solution.py:91
  343.4 3.1 gather_fusion.1
  346.5 2.5 bitcast_reduce_fusion
  (61 shorter events, 1.7 us)
Async XLA Ops:
  7.2 79.1 %copy-start = (bf16[96,448]{1,0:T(8,128)(2,1)S(1)}, bf16[96,448]{1,0:T(8,128)(2,1)}, u32[]{:S(2)}) copy-start(bf16[96,448]{1,0:T(8,128)(2,1)} %param.6) | copy-start | bytes 258052
  7.2 149.5 %all-gather.2.cloned.1.call-start = ((), (), s32[]{:S(2)}) async-start(), calls=%async_computation.2 | async-start | bytes 4587520 | tf_op jit(solution)/shard_map/all_gather | solution.py:62
  86.2 40.2 %copy-start.4 = (bf16[4,4,32,512]{3,2,1,0:T(8,128)(2,1)S(1)}, bf16[4,4,32,512]{3,2,1,0:T(8,128)(2,1)}, u32[]{:S(2)}) copy-start(bf16[4,4,32,512]{3,2,1,0:T(8,128)(2,1)} %param.10) | copy-start | bytes 1572868
  125.9 160.0 %all-reduce.3.cloned.1.call-start = ((), (), s32[]{:S(2)}) async-start(), calls=%async_computation.3 | async-start | bytes 7340032
  158.9 18.8 %slice-start.4 = ((s8[14680064]{0:T(1024)(128)(4,1)}), s8[4194304]{0:T(1024)(128)(4,1)S(1)}, s32[]{:S(2)}) async-start(s8[14680064]{0:T(1024)(128)(4,1)} %bitcast.202), calls=%async_computation.8 | async-start | bytes 8388608
  161.8 15.2 %slice-start = ((s8[14680064]{0:T(1024)(128)(4,1)}), s8[4194304]{0:T(1024)(128)(4,1)S(1)}, s32[]{:S(2)}) async-start(s8[14680064]{0:T(1024)(128)(4,1)} %bitcast.200), calls=%async_computation.4 | async-start | bytes 8388608
  161.8 16.0 %slice-start.5 = ((s8[14680064]{0:T(1024)(128)(4,1)}), s8[4194304]{0:T(1024)(128)(4,1)S(1)}, s32[]{:S(2)}) async-start(s8[14680064]{0:T(1024)(128)(4,1)} %bitcast.202), calls=%async_computation.9 | async-start | bytes 8388608
  164.7 12.3 %slice-start.1 = ((s8[14680064]{0:T(1024)(128)(4,1)}), s8[4194304]{0:T(1024)(128)(4,1)S(1)}, s32[]{:S(2)}) async-start(s8[14680064]{0:T(1024)(128)(4,1)} %bitcast.200), calls=%async_computation.5 | async-start | bytes 8388608
  168.6 8.4 %slice-start.2 = ((s8[14680064]{0:T(1024)(128)(4,1)}), s8[4194304]{0:T(1024)(128)(4,1)S(1)}, s32[]{:S(2)}) async-start(s8[14680064]{0:T(1024)(128)(4,1)} %bitcast.200), calls=%async_computation.6 | async-start | bytes 8388608
  168.7 8.4 %slice-start.3 = ((s8[14680064]{0:T(1024)(128)(4,1)}), s8[2097152]{0:T(1024)(128)(4,1)S(1)}, s32[]{:S(2)}) async-start(s8[14680064]{0:T(1024)(128)(4,1)} %bitcast.200), calls=%async_computation.7 | async-start | bytes 4194304
  168.7 9.1 %slice-start.6 = ((s8[14680064]{0:T(1024)(128)(4,1)}), s8[4194304]{0:T(1024)(128)(4,1)S(1)}, s32[]{:S(2)}) async-start(s8[14680064]{0:T(1024)(128)(4,1)} %bitcast.202), calls=%async_computation.10 | async-start | bytes 8388608
  174.2 3.6 %slice-start.7 = ((s8[14680064]{0:T(1024)(128)(4,1)}), s8[2097152]{0:T(1024)(128)(4,1)S(1)}, s32[]{:S(2)}) async-start(s8[14680064]{0:T(1024)(128)(4,1)} %bitcast.202), calls=%async_computation.11 | async-start | bytes 4194304
  197.9 6.0 %copy-start.2 = (f32[128,3584]{1,0:T(8,128)S(1)}, f32[128,3584]{1,0:T(8,128)}, u32[]{:S(2)}) copy-start(f32[128,3584]{1,0:T(8,128)} %fusion.23) | copy-start | bytes 5505028
  202.6 2.7 copy-start.3
  226.7 6.1 %copy-start.6 = (u32[32]{0:T(128)S(1)}, u32[32]{0:T(128)}, u32[]{:S(2)}) copy-start(u32[32]{0:T(128)} %constant.97) | copy-start | bytes 388
  226.7 13.8 %copy-start.5 = (f32[4]{0:T(128)S(1)}, f32[4]{0:T(128)}, u32[]{:S(2)}) copy-start(f32[4]{0:T(128)} %param.11) | copy-start | bytes 52
  297.5 36.7 %all-to-all-start.1 = ((bf16[8,2,28672]{2,1,0:T(2,128)(2,1)}), bf16[8,2,28672]{2,1,0:T(2,128)(2,1)S(1)}, u32[]{:S(2)}, u32[]{:S(2)}) async-start(bf16[8,2,28672]{2,1,0:T(2,128)(2,1)} %reshape.181), calls=%async_computation.1 | async-start | bytes 1835008 | tf_op jit(solution)/shard_map/all_to_all | solution.py:89
  343.4 5.6 %copy-start.1 = (bf16[96,448]{1,0:T(8,128)(2,1)S(1)}, bf16[96,448]{1,0:T(8,128)(2,1)}, u32[]{:S(2)}) copy-start(bf16[96,448]{1,0:T(8,128)(2,1)} %param.6) | copy-start | bytes 258052
Sparse Core Ops, SparseCore 0:
  126.1 30.5 all-gather.1
  208.8 77.1 all-reduce.2
where the time goes:
time: 356 us
  local copies, waits for them, and re-layouts  111 us (31%)
  waiting for transfers between devices  75.7 us (21%)
  matrix products  66.2 us (19%)
  blocking collectives  39.9 us (11%)
  other arithmetic  38.1 us (11%)
  between operations  19.7 us (6%)
  starting transfers between devices  5.77 us (2%)
    unnamed x3, waiting for transfers between devices  45.6 us
    scatter x1, local copies, waits for them, and re-layouts, slot_tables(): jnp.zeros((experts, capacity), jnp.bool_).at[flat_routes, slot_ranks]  38.1 us
    scatter x1, local copies, waits for them, and re-layouts, slot_tables(): jnp.zeros((experts, capacity), jnp.int32).at[flat_routes, slot_ranks]  37.4 us
    all_to_all x1, blocking collectives, body(): lax.all_to_all(outgoing, 'expert', split_axis=0, concat_axis=3, tiled=True)  32.8 us
    convert_element_type x1, other arithmetic, body(): (clip_scale[:, None, None] * jnp.stack(up_list)).astype(jnp.bfloat16)  30.4 us
    all_gather x1, waiting for transfers between devices, body(): gathered = lax.all_gather(arrived, 'dp', axis=1, tiled=True)  30.2 us
    dot_general x4, matrix products, expert_math(): lax.dot_general(row_block, gate_act, over_rows, preferred_element_type=jn...  19.7 us
    dot_general x4, matrix products, expert_math(): lax.dot_general(row_block, up_act, over_rows, preferred_element_type=jnp....  18.9 us
  transfers between devices with their start and end apart: 3, of which 2 were waited for; matrix products, arithmetic and copies ran while one was open for 14% of the time, Pallas kernels for 0%

commit v1 on v0

--- a/solution.py
+++ b/solution.py
@@ -1,6 +1,10 @@
+import functools
+
 import jax
 import jax.numpy as jnp
 from jax import lax
+from jax.experimental import pallas as pl
+from jax.experimental.pallas import tpu as pltpu
 from jax.sharding import PartitionSpec as P
 
 
@@ -41,7 +45,7 @@
     return (hidden_rows, raw_gate, raw_up, partial_value)
 
 
-def body(tokens, routes, gate_weight, up_weight, hidden_grad, clip_limit):
+def plain_body(tokens, routes, gate_weight, up_weight, hidden_grad, clip_limit):
     dp_count = lax.axis_size("dp")
     expert_count = lax.axis_size("expert")
     local_experts = gate_weight.shape[0]
@@ -95,6 +99,449 @@
     return (hidden, grad_gate, grad_up, token_grad)
 
 
+VMEM_LIMIT = 60 * 1024 * 1024
+F32 = jnp.float32
+BF16 = jnp.bfloat16
+Z_COUNT = 4
+
+
+def flip(bit, by):
+    return bit + by - 2 * bit * by
+
+
+class Place:
+    def __init__(self):
+        self.dp = lax.axis_index("dp")
+        self.ex = lax.axis_index("expert")
+        self.y, self.k = self.dp // 2, self.dp % 2
+        self.z, self.x = self.ex // 2, self.ex % 2
+
+    def z_at(self, j):
+        return 2 * flip(self.z // 2, j // 2) + flip(self.z % 2, j % 2)
+
+    def unit(self, core, s, f, j):
+        xx = flip(self.x, f * (1 - core) + s * core)
+        yy = flip(self.y, s * (1 - core) + f * core)
+        return (2 * self.z_at(j) + xx) * 4 + 2 * yy + core
+
+    def sibling(self):
+        return (2 * self.y + 1 - self.k, self.ex)
+
+    def second(self):
+        return (2 * flip(self.y, 1 - self.k) + self.k, 2 * self.z + flip(self.x, self.k))
+
+    def first(self):
+        return (2 * flip(self.y, self.k) + self.k, 2 * self.z + flip(self.x, 1 - self.k))
+
+    def along_z(self, j):
+        return (self.dp, 2 * self.z_at(j) + self.x)
+
+    def across(self):
+        return (3 - self.dp, self.ex)
+
+    def other_y(self):
+        return (2 * (1 - self.y) + self.k, self.ex)
+
+    def enter(self):
+        barrier = pltpu.get_barrier_semaphore()
+        partners = [self.sibling(), self.first(), self.second(), self.across()]
+        partners += [self.along_z(j) for j in range(1, Z_COUNT)]
+        for partner in partners:
+            pl.semaphore_signal(
+                barrier, inc=1, device_id=partner, device_id_type=pl.DeviceIdType.MESH
+            )
+        pl.semaphore_wait(barrier, len(partners))
+
+
+def label(s, f, j):
+    return s * 8 + f * 4 + j
+
+
+class Gather:
+    def __init__(self, place, units, send_sem, recv_sem):
+        self.place, self.units = place, units
+        self.send_sem, self.recv_sem = send_sem, recv_sem
+        self.sent = []
+
+    def copy(self, unit, device, send_index, recv_index):
+        return pltpu.make_async_remote_copy(
+            src_ref=self.units.at[unit],
+            dst_ref=self.units.at[unit],
+            send_sem=self.send_sem.at[send_index],
+            recv_sem=self.recv_sem.at[recv_index],
+            device_id=device,
+            device_id_type=pl.DeviceIdType.MESH,
+        )
+
+    def send(self, unit, device, recv_index):
+        copy = self.copy(unit, device, len(self.sent), recv_index)
+        copy.start()
+        self.sent.append(copy)
+
+    def arrive(self, unit, recv_index):
+        self.copy(unit, self.place.sibling(), 0, recv_index).wait_recv()
+
+    def forward(self, s, f, j):
+        place = self.place
+        unit = place.unit(place.k, s, f, j)
+        if (s, f, j) != (0, 0, 0):
+            self.arrive(unit, label(s, f, j))
+        if s == 0:
+            self.send(unit, place.second(), label(1, f, j))
+        if s == 0 and f == 0:
+            self.send(unit, place.first(), label(0, 1, j))
+        if (s, f, j) == (0, 0, 0):
+            for j_to in range(1, Z_COUNT):
+                self.send(unit, place.along_z(j_to), label(0, 0, j_to))
+        self.send(unit, place.sibling(), 16 + label(s, f, j))
+
+    def from_sibling(self, s, f, j):
+        self.arrive(self.place.unit(1 - self.place.k, s, f, j), 16 + label(s, f, j))
+
+    def finish(self):
+        for copy in self.sent:
+            copy.wait_send()
+
+
+def gather_kernel(tokens_ref, units_ref, send_sem, recv_sem):
+    place = Place()
+    place.enter()
+    units_ref[place.unit(place.k, 0, 0, 0)] = tokens_ref[...]
+    gather = Gather(place, units_ref, send_sem, recv_sem)
+    for j in range(Z_COUNT):
+        gather.forward(0, 0, j)
+        gather.forward(0, 1, j)
+    for j in range(Z_COUNT):
+        gather.forward(1, 0, j)
+        gather.forward(1, 1, j)
+    for j in range(Z_COUNT):
+        for s in range(2):
+            for f in range(2):
+                gather.from_sibling(s, f, j)
+    gather.finish()
+
+
+def one_hot_rows(routes_ref, first_expert, experts, capacity, block_rows):
+    tokens = routes_ref.shape[1]
+    blocks = tokens // block_rows
+    routes = routes_ref[...]
+    masks = [
+        jnp.sum((routes == first_expert + e).astype(F32), axis=0, keepdims=True)
+        for e in range(experts)
+    ]
+    mask = jnp.concatenate(masks + [jnp.zeros((8 - experts, tokens), F32)], axis=0)
+    earlier = lax.broadcasted_iota(jnp.int32, (tokens, tokens), 0)
+    later = lax.broadcasted_iota(jnp.int32, (tokens, tokens), 1)
+    block_start = jnp.zeros((tokens, tokens), jnp.int32)
+    slot_start = jnp.zeros((8, tokens), jnp.int32)
+    token = lax.broadcasted_iota(jnp.int32, (8, tokens), 1)
+    for b in range(1, blocks):
+        block_start = jnp.where(later >= b * block_rows, b * block_rows, block_start)
+        slot_start = jnp.where(token >= b * block_rows, b * capacity, slot_start)
+    counted = jnp.where((earlier < later) & (earlier >= block_start), 1.0, 0.0).astype(BF16)
+    rank = jnp.dot(mask.astype(BF16), counted, preferred_element_type=F32)
+    slot = jnp.where(mask > 0.5, rank + slot_start.astype(F32), -1.0)
+    rows = lax.broadcasted_iota(jnp.int32, (blocks * capacity, tokens), 0).astype(F32)
+    return jnp.concatenate(
+        [jnp.where(rows == slot[e : e + 1], 1.0, 0.0).astype(BF16) for e in range(experts)], axis=0
+    )
+
+
+OVER_LANES = (((1,), (1,)), ((), ()))
+OVER_ROWS = (((0,), (0,)), ((), ()))
+
+
+def dot(a, b, dims=(((1,), (0,)), ((), ()))):
+    return lax.dot_general(a, b, dims, preferred_element_type=F32)
+
+
+def start_weights(gate_hbm, up_hbm, gate_v, up_v, weight_sem, chunk):
+    width = gate_hbm.shape[1] // weight_sem.shape[1]
+    rows = pl.ds(chunk * width, width)
+    copies = [
+        pltpu.make_async_copy(gate_hbm.at[:, rows], gate_v.at[:, rows], weight_sem.at[0, chunk]),
+        pltpu.make_async_copy(up_hbm.at[:, rows], up_v.at[:, rows], weight_sem.at[1, chunk]),
+    ]
+    return copies
+
+
+def activate(e, acc_ref, grad_ref, hidden_ref, act_ref):
+    units = grad_ref.shape[2]
+    gate_pre = acc_ref[e, :, :units]
+    up_pre = acc_ref[e, :, units:]
+    sigma = jax.nn.sigmoid(gate_pre)
+    grad = grad_ref[e].astype(F32)
+    hidden_ref[e] = (gate_pre * sigma * up_pre).astype(BF16)
+    act_ref[e, :, units:] = (grad * gate_pre * sigma).astype(BF16)
+    act_ref[e, :, :units] = (grad * up_pre * sigma * (1.0 + gate_pre * (1.0 - sigma))).astype(BF16)
+
+
+def expert_kernel(
+    routes_ref, units_ref, grad_ref, gate_hbm, up_hbm,
+    hidden_ref, act_ref, rows_ref, sums_ref, square_ref,
+    gate_v, up_v, onehot_ref, acc_ref, gram_ref, back_ref, weight_sem,
+):
+    experts, slots, units = grad_ref.shape
+    chunks = rows_ref.shape[0]
+    width = rows_ref.shape[2]
+    d_count = units_ref.shape[0] // chunks
+    block_rows = units_ref.shape[1]
+    tokens = d_count * block_rows
+    for chunk in range(chunks):
+        for copy in start_weights(gate_hbm, up_hbm, gate_v, up_v, weight_sem, chunk):
+            copy.start()
+    first_expert = lax.axis_index("expert") * experts
+    onehot = one_hot_rows(routes_ref, first_expert, experts, slots // d_count, block_rows)
+    onehot_ref[...] = onehot
+    back_ref[...] = onehot.T
+    acc_ref[...] = jnp.zeros_like(acc_ref)
+    gram_ref[...] = jnp.zeros_like(gram_ref)
+
+    def forward(chunk, carry):
+        for copy in start_weights(gate_hbm, up_hbm, gate_v, up_v, weight_sem, chunk):
+            copy.wait()
+        here = units_ref[pl.ds(chunk * d_count, d_count)].reshape(tokens, width)
+        rows_ref[chunk] = dot(onehot_ref[...], here).astype(BF16)
+        span = pl.ds(pl.multiple_of(chunk * width, 64), width)
+        for e in range(experts):
+            mine = rows_ref[chunk, e * slots : (e + 1) * slots]
+            acc_ref[e, :, :units] += dot(mine, gate_v[e, span])
+            acc_ref[e, :, units:] += dot(mine, up_v[e, span])
+            gram_ref[e] += dot(mine, mine, OVER_LANES)
+        return carry
+
+    lax.fori_loop(0, chunks, forward, 0)
+    squares = []
+    for e in range(experts):
+        activate(e, acc_ref, grad_ref, hidden_ref, act_ref)
+        act = act_ref[e]
+        product = dot(act, act, OVER_LANES) * gram_ref[e]
+        squares.append(jnp.sum(jnp.sum(product, axis=0, keepdims=True), axis=1, keepdims=True))
+    squares.append(jnp.zeros((8 - experts, 1), F32))
+    square_ref[...] = jnp.broadcast_to(jnp.concatenate(squares, axis=0), square_ref.shape)
+
+    def backward(chunk, carry):
+        span = pl.ds(pl.multiple_of(chunk * width, 64), width)
+        parts = []
+        for e in range(experts):
+            part = dot(act_ref[e, :, :units], gate_v[e, span], OVER_LANES)
+            part = part + dot(act_ref[e, :, units:], up_v[e, span], OVER_LANES)
+            parts.append(part.astype(BF16))
+        total = dot(back_ref[...], jnp.concatenate(parts, axis=0))
+        sums_ref[pl.ds(chunk * d_count, d_count)] = total.astype(BF16).reshape(
+            d_count, block_rows, width
+        )
+        return carry
+
+    lax.fori_loop(0, chunks, backward, 0)
+
+
+class Scatter:
+    def __init__(self, place, sums, work, buffers, send_sem, recv_sem):
+        self.place, self.sums, self.work = place, sums, work
+        self.buffers = buffers
+        self.send_sem, self.recv_sem = send_sem, recv_sem
+        self.sent = []
+
+    def copy(self, src, dst, device, send_index, recv_index):
+        return pltpu.make_async_remote_copy(
+            src_ref=src,
+            dst_ref=dst,
+            send_sem=self.send_sem.at[send_index],
+            recv_sem=self.recv_sem.at[recv_index],
+            device_id=device,
+            device_id_type=pl.DeviceIdType.MESH,
+        )
+
+    def send(self, src, slot, device):
+        copy = self.copy(src, self.buffers.at[slot], device, len(self.sent), slot)
+        copy.start()
+        self.sent.append(copy)
+
+    def take(self, slot):
+        place = self.place
+        landed = self.buffers.at[slot]
+        self.copy(landed, landed, place.sibling(), 0, slot).wait_recv()
+        return self.buffers[slot].astype(F32)
+
+    def to_sibling(self, s, f, j):
+        place = self.place
+        unit = place.unit(1 - place.k, s, f, j)
+        self.send(self.sums.at[unit], label(s, f, j), place.sibling())
+
+    def collect(self, s, f, j):
+        place = self.place
+        total = self.sums[place.unit(place.k, s, f, j)].astype(F32)
+        total = total + self.take(label(s, f, j))
+        if s == 0:
+            total = total + self.take(16 + f * 4 + j)
+        if s == 0 and f == 0:
+            total = total + self.take(24 + j)
+        return total
+
+    def pass_on(self, s, f, j):
+        place = self.place
+        held = label(s, f, j)
+        self.work[held] = self.collect(s, f, j).astype(BF16)
+        if s == 1:
+            self.send(self.work.at[held], 16 + f * 4 + j, place.second())
+        elif f == 1:
+            self.send(self.work.at[held], 24 + j, place.first())
+        else:
+            self.send(self.work.at[held], 27 + j, place.along_z(j))
+
+    def finish(self):
+        for copy in self.sent:
+            copy.wait_send()
+
+
+def scatter_kernel(
+    sums_ref, square_ref, token_ref, squares_ref,
+    work, buffers, square_buf, send_sem, recv_sem, square_send, square_recv,
+):
+    place = Place()
+    place.enter()
+    scatter = Scatter(place, sums_ref, work, buffers, send_sem, recv_sem)
+    others = [place.sibling(), place.other_y(), place.across()]
+    square_copies = []
+    for i, other in enumerate(others):
+        copy = pltpu.make_async_remote_copy(
+            src_ref=square_ref,
+            dst_ref=square_buf.at[i],
+            send_sem=square_send.at[i],
+            recv_sem=square_recv.at[i],
+            device_id=other,
+            device_id_type=pl.DeviceIdType.MESH,
+        )
+        copy.start()
+        square_copies.append(copy)
+    order = [(s, f) for s in (1, 0) for f in (1, 0)]
+    for s, f in order:
+        for j in (1, 2, 3, 0):
+            scatter.to_sibling(s, f, j)
+    for s, f in order:
+        for j in (1, 2, 3, 0):
+            if (s, f, j) != (0, 0, 0):
+                scatter.pass_on(s, f, j)
+    total = scatter.collect(0, 0, 0)
+    for j in range(1, Z_COUNT):
+        total = total + scatter.take(27 + j)
+    token_ref[...] = total.astype(BF16)
+    squares = square_ref[...]
+    for i, copy in enumerate(square_copies):
+        copy.wait()
+        squares = squares + square_buf[i]
+    squares_ref[...] = squares
+    scatter.finish()
+
+
+def weight_grad_kernel(count, scale_ref, rows_ref, act_ref, gate_ref, up_ref):
+    width = rows_ref.shape[2]
+    units = gate_ref.shape[2]
+    scale = scale_ref[pl.program_id(0)]
+    for chunk in range(count):
+        raw = dot(rows_ref[chunk], act_ref[0], OVER_ROWS) * scale
+        gate_ref[0, chunk * width : (chunk + 1) * width] = raw[:, :units].astype(BF16)
+        up_ref[0, chunk * width : (chunk + 1) * width] = raw[:, units:].astype(BF16)
+
+
+def whole_vmem(count):
+    return [pl.BlockSpec(memory_space=pltpu.VMEM)] * count
+
+
+def kernel_body(tokens, routes, gate_weight, up_weight, hidden_grad, clip_limit):
+    chunks = lax.axis_size("expert")
+    d_count = lax.axis_size("dp")
+    experts, model_width, hidden_units = gate_weight.shape
+    block_rows, width = tokens.shape
+    capacity = hidden_grad.shape[2]
+    slots = d_count * capacity
+    all_units = chunks * d_count
+    token_rows = d_count * block_rows
+    units = pl.pallas_call(
+        gather_kernel,
+        out_shape=jax.ShapeDtypeStruct((all_units, block_rows, width), BF16),
+        in_specs=whole_vmem(1),
+        out_specs=whole_vmem(1)[0],
+        scratch_shapes=[pltpu.SemaphoreType.DMA((31,)), pltpu.SemaphoreType.DMA((32,))],
+        compiler_params=pltpu.CompilerParams(
+            collective_id=0, has_side_effects=True, vmem_limit_bytes=VMEM_LIMIT
+        ),
+        name="gather_tokens",
+    )(tokens)
+    hidden, act, rows, sums, square = pl.pallas_call(
+        expert_kernel,
+        out_shape=[
+            jax.ShapeDtypeStruct((experts, slots, hidden_units), BF16),
+            jax.ShapeDtypeStruct((experts, slots, 2 * hidden_units), BF16),
+            jax.ShapeDtypeStruct((chunks, experts * slots, width), BF16),
+            jax.ShapeDtypeStruct((all_units, block_rows, width), BF16),
+            jax.ShapeDtypeStruct((8, 128), F32),
+        ],
+        in_specs=whole_vmem(3) + [pl.BlockSpec(memory_space=pl.ANY)] * 2,
+        out_specs=whole_vmem(5),
+        scratch_shapes=[
+            pltpu.VMEM((experts, model_width, hidden_units), BF16),
+            pltpu.VMEM((experts, model_width, hidden_units), BF16),
+            pltpu.VMEM((experts * slots, token_rows), BF16),
+            pltpu.VMEM((experts, slots, 2 * hidden_units), F32),
+            pltpu.VMEM((experts, slots, slots), F32),
+            pltpu.VMEM((token_rows, experts * slots), BF16),
+            pltpu.SemaphoreType.DMA((2, chunks)),
+        ],
+        compiler_params=pltpu.CompilerParams(vmem_limit_bytes=VMEM_LIMIT),
+        name="experts",
+    )(routes.T, units, hidden_grad.reshape(experts, slots, hidden_units), gate_weight, up_weight)
+    token_grad, squares = pl.pallas_call(
+        scatter_kernel,
+        out_shape=[
+            jax.ShapeDtypeStruct((block_rows, width), BF16),
+            jax.ShapeDtypeStruct((8, 128), F32),
+        ],
+        in_specs=whole_vmem(2),
+        out_specs=whole_vmem(2),
+        scratch_shapes=[
+            pltpu.VMEM((16, block_rows, width), BF16),
+            pltpu.VMEM((31, block_rows, width), BF16),
+            pltpu.VMEM((3, 8, 128), F32),
+            pltpu.SemaphoreType.DMA((31,)),
+            pltpu.SemaphoreType.DMA((31,)),
+            pltpu.SemaphoreType.DMA((3,)),
+            pltpu.SemaphoreType.DMA((3,)),
+        ],
+        compiler_params=pltpu.CompilerParams(
+            collective_id=1, has_side_effects=True, vmem_limit_bytes=VMEM_LIMIT
+        ),
+        name="scatter_grads",
+    )(sums, square)
+    grad_gate, grad_up = weight_grads(rows, act, squares, clip_limit, gate_weight.shape, d_count)
+    return (hidden.reshape(hidden_grad.shape), grad_gate, grad_up, token_grad)
+
+
+def weight_grads(rows, act, squares, clip_limit, shape, d_count):
+    experts, model_width, hidden_units = shape
+    chunks, _, width = rows.shape
+    slots = act.shape[1]
+    mean = squares[:experts, 0] / (2.0 * model_width * hidden_units * d_count)
+    scale = jnp.minimum(1.0, clip_limit / jnp.sqrt(mean + 1e-06))
+    halves = 2
+    count = chunks // halves
+    out_block = pl.BlockSpec((1, count * width, hidden_units), lambda e, h: (e, h, 0))
+    return pl.pallas_call(
+        functools.partial(weight_grad_kernel, count),
+        grid=(experts, halves),
+        out_shape=[jax.ShapeDtypeStruct(shape, BF16)] * 2,
+        in_specs=[
+            pl.BlockSpec(memory_space=pltpu.SMEM),
+            pl.BlockSpec((count, slots, width), lambda e, h: (h, e, 0)),
+            pl.BlockSpec((1, slots, 2 * hidden_units), lambda e, h: (e, 0, 0)),
+        ],
+        out_specs=[out_block, out_block],
+        compiler_params=pltpu.CompilerParams(vmem_limit_bytes=VMEM_LIMIT),
+        name="weight_grads",
+    )(scale, rows, act)
+
+
 def solution(mesh):
     placed = (
         P("dp", "expert"),
@@ -104,8 +551,9 @@
         P("expert", None, None, "dp"),
         P("expert"),
     )
+    fits = mesh.shape["dp"] == 4 and mesh.shape["expert"] == 2 * Z_COUNT
     return jax.shard_map(
-        body,
+        kernel_body if fits else plain_body,
         mesh=mesh,
         in_specs=placed,
         out_specs=(

time: 356 us -> 103 us (0.29)
  local copies, waits for them, and re-layouts: 111 us -> 1.54 us
  Pallas kernels: 0 us -> 99.5 us
  waiting for transfers between devices: 75.7 us -> 0 us
  matrix products: 66.2 us -> 0 us
  blocking collectives: 39.9 us -> 0 us
  other arithmetic: 38.1 us -> 1.31 us
  between operations: 19.7 us -> 0.67 us
  starting transfers between devices: 5.77 us -> 0 us
    pallas_call x0 -> x4, Pallas kernels: none -> 99.5 us  [the longest x1 31 us: kernel_body(): pl.pallas_call(gather_kernel, out_shape=jax.ShapeDtypeStruct((all_units,...]
    scatter x2 -> x0, local copies, waits for them, and re-layouts: 75.5 us -> none  [the longest x1 38.1 us: slot_tables(): jnp.zeros((experts, capacity), jnp.bool_).at[flat_routes, slot_ranks]]
    dot_general x24 -> x0, matrix products: 66.2 us -> none  [the longest x4 19.7 us: expert_math(): lax.dot_general(row_block, gate_act, over_rows, preferred_element_type=jn...]
    unnamed x3 -> x0, waiting for transfers between devices: 45.6 us -> none
    all_to_all x1 -> x0, blocking collectives: 32.8 us -> none  [body(): lax.all_to_all(outgoing, 'expert', split_axis=0, concat_axis=3, tiled=True)]
    convert_element_type x2 -> x0, other arithmetic: 30.4 us -> none  [the longest x1 30.4 us: body(): (clip_scale[:, None, None] * jnp.stack(up_list)).astype(jnp.bfloat16)]
    all_gather x1 -> x0, waiting for transfers between devices: 30.2 us -> none  [body(): gathered = lax.all_gather(arrived, 'dp', axis=1, tiled=True)]
    unnamed x35 -> x3, local copies, waits for them, and re-layouts: 12.4 us -> 1.54 us
  transfers between devices with their start and end apart: 3 -> 0, of which waited for: 2 -> 0; matrix products, arithmetic and copies ran while one was open for 14% -> 0% of each run, Pallas kernels for 0% -> 0%
where the time goes in v1:
time: 103 us
  Pallas kernels  99.5 us (97%)
  local copies, waits for them, and re-layouts  1.54 us (1%)
  other arithmetic  1.31 us (1%)
    pallas_call x1, Pallas kernels, kernel_body(): pl.pallas_call(gather_kernel, out_shape=jax.ShapeDtypeStruct((all_units,...  31 us
    pallas_call x1, Pallas kernels, kernel_body(): pl.pallas_call(expert_kernel, out_shape=[jax.ShapeDtypeStruct((experts, s...  28.3 us
    pallas_call x1, Pallas kernels, kernel_body(): pl.pallas_call(scatter_kernel, out_shape=[jax.ShapeDtypeStruct((block_row...  26.3 us
    pallas_call x1, Pallas kernels, weight_grads(): pl.pallas_call(functools.partial(weight_grad_kernel, count), grid=(expert...  13.9 us

profile of v1, /device:TPU:0, one launch (start us, length us, event | category | flops | bytes accessed | tf_op | source)
XLA Modules:
  0.0 103.0 jit_solution(6992713523409613469)
XLA Ops:
  0.6 31.0 %gather_tokens.1.units_ref = bf16[32,96,448]{2,1,0:T(8,128)(2,1)} custom-call(bf16[96,448]{1,0:T(8,128)(2,1)} %tokens_ref.1), custom_call_target="tpu_custom_call" | custom-call | tf_op jit(solution)/shard_map/gather_tokens/pallas_call | solution.py:461
  31.7 0.0 copy-start
  31.7 28.3 %experts.1 = (bf16[4,128,512]{2,1,0:T(8,128)(2,1)}, bf16[4,128,1024]{2,1,0:T(8,128)(2,1)}, bf16[8,512,448]{2,1,0:T(8,128)(2,1)}, bf16[32,96,448]{2,1,0:T(8,128)(2,1)}, f32[8,128]{1,0:T(8,128)}) custom-call(s32[8,384]{1,0:T(8,128)} %bitcast.4, bf16[32,96,448]{2,1,0:T(8,128)(2,1)} %gather_tokens.1.units_ref, bf16[4,128,512]{2,1,0:T(8,128)(2,1)} %bitcast.3, ...), custom_call_target="tpu_custom_call" | custom-call | tf_op jit(solution)/shard_map/experts/pallas_call | solution.py:472
  59.9 26.3 %scatter_grads.1 = (bf16[96,448]{1,0:T(8,128)(2,1)}, f32[8,128]{1,0:T(8,128)}) custom-call(bf16[32,96,448]{2,1,0:T(8,128)(2,1)} %get-tuple-element.14.sums_ref, f32[8,128]{1,0:T(8,128)} %get-tuple-element.15.square_ref), custom_call_target="tpu_custom_call" | custom-call | tf_op jit(solution)/shard_map/scatter_grads/pallas_call | solution.py:495
  86.2 0.8 rsqrt_reduce_fusion
  87.0 0.0 copy-done
  87.0 0.5 multiply_minimum_fusion.scale_ref
  87.6 13.9 %weight_grads.1 = (bf16[4,3584,512]{2,1,0:T(8,128)(2,1)}, bf16[4,3584,512]{2,1,0:T(8,128)(2,1)}) custom-call(f32[4]{0:T(128)} %multiply_minimum_fusion.scale_ref, bf16[8,512,448]{2,1,0:T(8,128)(2,1)} %get-tuple-element.17.rows_ref, bf16[4,128,1024]{2,1,0:T(8,128)(2,1)} %get-tuple-element.18.act_ref), custom_call_target="tpu_custom_call" | custom-call | tf_op jit(solution)/shard_map/weight_grads/pallas_call | solution.py:530
  101.5 1.5 %copy.11 = bf16[96,448]{1,0:T(8,128)(2,1)} copy(bf16[96,448]{1,0:T(8,128)(2,1)} %get-tuple-element.29) | data formatting | bytes 172032
Async XLA Ops:
  31.7 55.4 %copy-start = (f32[4]{0:T(128)S(1)}, f32[4]{0:T(128)}, u32[]{:S(2)}) copy-start(f32[4]{0:T(128)} %param.11) | copy-start | bytes 52

commit v2 on v1

--- a/solution.py
+++ b/solution.py
@@ -161,7 +161,6 @@
     def __init__(self, place, units, send_sem, recv_sem):
         self.place, self.units = place, units
         self.send_sem, self.recv_sem = send_sem, recv_sem
-        self.sent = []
 
     def copy(self, unit, device, send_index, recv_index):
         return pltpu.make_async_remote_copy(
@@ -173,52 +172,32 @@
             device_id_type=pl.DeviceIdType.MESH,
         )
 
-    def send(self, unit, device, recv_index):
-        copy = self.copy(unit, device, len(self.sent), recv_index)
-        copy.start()
-        self.sent.append(copy)
-
     def arrive(self, unit, recv_index):
         self.copy(unit, self.place.sibling(), 0, recv_index).wait_recv()
 
-    def forward(self, s, f, j):
+    def forward(self, s, f, j, own=False):
         place = self.place
         unit = place.unit(place.k, s, f, j)
-        if (s, f, j) != (0, 0, 0):
+        if not own:
             self.arrive(unit, label(s, f, j))
         if s == 0:
-            self.send(unit, place.second(), label(1, f, j))
+            self.copy(unit, place.second(), f * 4 + j, label(1, f, j)).start()
         if s == 0 and f == 0:
-            self.send(unit, place.first(), label(0, 1, j))
-        if (s, f, j) == (0, 0, 0):
-            for j_to in range(1, Z_COUNT):
-                self.send(unit, place.along_z(j_to), label(0, 0, j_to))
-        self.send(unit, place.sibling(), 16 + label(s, f, j))
-
-    def from_sibling(self, s, f, j):
-        self.arrive(self.place.unit(1 - self.place.k, s, f, j), 16 + label(s, f, j))
+            self.copy(unit, place.first(), 8 + j, label(0, 1, j)).start()
+        if own:
+            for to in range(1, Z_COUNT):
+                self.copy(unit, place.along_z(to), 11 + to, label(0, 0, to)).start()
+        held = label(s, f, j)
+        self.copy(unit, place.sibling(), 15 + held, 16 + held).start()
+
+    def from_sibling(self, xf, yf, j):
+        core = 1 - self.place.k
+        s, f = xf * core + yf * (1 - core), xf * (1 - core) + yf * core
+        self.arrive(self.place.unit(core, s, f, j), 16 + label(s, f, j))
 
     def finish(self):
-        for copy in self.sent:
-            copy.wait_send()
-
-
-def gather_kernel(tokens_ref, units_ref, send_sem, recv_sem):
-    place = Place()
-    place.enter()
-    units_ref[place.unit(place.k, 0, 0, 0)] = tokens_ref[...]
-    gather = Gather(place, units_ref, send_sem, recv_sem)
-    for j in range(Z_COUNT):
-        gather.forward(0, 0, j)
-        gather.forward(0, 1, j)
-    for j in range(Z_COUNT):
-        gather.forward(1, 0, j)
-        gather.forward(1, 1, j)
-    for j in range(Z_COUNT):
-        for s in range(2):
-            for f in range(2):
-                gather.from_sibling(s, f, j)
-    gather.finish()
+        for i in range(31):
+            self.copy(self.place.unit(self.place.k, 0, 0, 0), self.place.sibling(), i, 0).wait_send()
 
 
 def one_hot_rows(routes_ref, first_expert, experts, capacity, block_rows):
@@ -276,10 +255,64 @@
     act_ref[e, :, :units] = (grad * up_pre * sigma * (1.0 + gate_pre * (1.0 - sigma))).astype(BF16)
 
 
+class Scatter:
+    def __init__(self, place, sums, work, buffers, send_sem, recv_sem):
+        self.place, self.sums, self.work = place, sums, work
+        self.buffers = buffers
+        self.send_sem, self.recv_sem = send_sem, recv_sem
+
+    def copy(self, src, slot, device):
+        return pltpu.make_async_remote_copy(
+            src_ref=src,
+            dst_ref=self.buffers.at[slot],
+            send_sem=self.send_sem.at[slot],
+            recv_sem=self.recv_sem.at[slot],
+            device_id=device,
+            device_id_type=pl.DeviceIdType.MESH,
+        )
+
+    def take(self, slot):
+        self.copy(self.buffers.at[slot], slot, self.place.sibling()).wait_recv()
+        return self.buffers[slot].astype(F32)
+
+    def to_sibling(self, xf, j):
+        place = self.place
+        core = 1 - place.k
+        for yf in range(2):
+            s, f = xf * core + yf * (1 - core), xf * (1 - core) + yf * core
+            unit = place.unit(core, s, f, j)
+            self.copy(self.sums.at[unit], label(s, f, j), place.sibling()).start()
+
+    def collect(self, s, f, j):
+        place = self.place
+        total = self.sums[place.unit(place.k, s, f, j)].astype(F32)
+        total = total + self.take(label(s, f, j))
+        if s == 0:
+            total = total + self.take(16 + f * 4 + j)
+        if s == 0 and f == 0:
+            total = total + self.take(24 + j)
+        return total
+
+    def pass_on(self, s, f, j):
+        place = self.place
+        held = label(s, f, j)
+        self.work[held] = self.collect(s, f, j).astype(BF16)
+        if s == 1:
+            self.copy(self.work.at[held], 16 + f * 4 + j, place.second()).start()
+        else:
+            self.copy(self.work.at[held], 24 + j, place.first()).start()
+
+    def finish(self):
+        for slot in range(28):
+            self.copy(self.buffers.at[slot], slot, self.place.sibling()).wait_send()
+
+
 def expert_kernel(
-    routes_ref, units_ref, grad_ref, gate_hbm, up_hbm,
-    hidden_ref, act_ref, rows_ref, sums_ref, square_ref,
-    gate_v, up_v, onehot_ref, acc_ref, gram_ref, back_ref, weight_sem,
+    tokens_ref, routes_ref, grad_ref, limit_ref, gate_hbm, up_hbm,
+    hidden_ref, act_ref, rows_ref, scale_ref, total_ref,
+    units_ref, sums_ref, gate_v, up_v, onehot_ref, acc_ref, gram_ref, back_ref,
+    work, buffers, square_ref, square_buf,
+    weight_sem, gather_send, gather_recv, scatter_send, scatter_recv, square_send, square_recv,
 ):
     experts, slots, units = grad_ref.shape
     chunks = rows_ref.shape[0]
@@ -287,18 +320,42 @@
     d_count = units_ref.shape[0] // chunks
     block_rows = units_ref.shape[1]
     tokens = d_count * block_rows
-    for chunk in range(chunks):
-        for copy in start_weights(gate_hbm, up_hbm, gate_v, up_v, weight_sem, chunk):
-            copy.start()
-    first_expert = lax.axis_index("expert") * experts
+    place = Place()
+
+    def chunk_at(xf, j):
+        return 2 * place.z_at(j) + flip(place.x, xf)
+
+    def weights(chunk):
+        return start_weights(gate_hbm, up_hbm, gate_v, up_v, weight_sem, chunk)
+
+    for j in range(Z_COUNT):
+        for xf in range(2):
+            for copy in weights(chunk_at(xf, j)):
+                copy.start()
+    units_ref[place.unit(place.k, 0, 0, 0)] = tokens_ref[...]
+    place.enter()
+    gather = Gather(place, units_ref, gather_send, gather_recv)
+    gather.forward(0, 0, 0, own=True)
+
+    first_expert = place.ex * experts
     onehot = one_hot_rows(routes_ref, first_expert, experts, slots // d_count, block_rows)
     onehot_ref[...] = onehot
     back_ref[...] = onehot.T
     acc_ref[...] = jnp.zeros_like(acc_ref)
     gram_ref[...] = jnp.zeros_like(gram_ref)
 
-    def forward(chunk, carry):
-        for copy in start_weights(gate_hbm, up_hbm, gate_v, up_v, weight_sem, chunk):
+    for j in range(Z_COUNT):
+        if j > 0:
+            gather.forward(0, 0, j)
+        gather.forward(0, 1, j)
+    gather.forward(1, 0, 0)
+    gather.forward(1, 1, 0)
+
+    def multiply(xf, j):
+        chunk = chunk_at(xf, j)
+        gather.from_sibling(xf, 0, j)
+        gather.from_sibling(xf, 1, j)
+        for copy in weights(chunk):
             copy.wait()
         here = units_ref[pl.ds(chunk * d_count, d_count)].reshape(tokens, width)
         rows_ref[chunk] = dot(onehot_ref[...], here).astype(BF16)
@@ -308,9 +365,19 @@
             acc_ref[e, :, :units] += dot(mine, gate_v[e, span])
             acc_ref[e, :, units:] += dot(mine, up_v[e, span])
             gram_ref[e] += dot(mine, mine, OVER_LANES)
+
+    def forward(j, carry):
+        multiply(0, j)
+
+        @pl.when(j < Z_COUNT - 1)
+        def _():
+            gather.forward(1, 0, j + 1)
+            gather.forward(1, 1, j + 1)
+
+        multiply(1, j)
         return carry
 
-    lax.fori_loop(0, chunks, forward, 0)
+    lax.fori_loop(0, Z_COUNT, forward, 0)
     squares = []
     for e in range(experts):
         activate(e, acc_ref, grad_ref, hidden_ref, act_ref)
@@ -319,8 +386,23 @@
         squares.append(jnp.sum(jnp.sum(product, axis=0, keepdims=True), axis=1, keepdims=True))
     squares.append(jnp.zeros((8 - experts, 1), F32))
     square_ref[...] = jnp.broadcast_to(jnp.concatenate(squares, axis=0), square_ref.shape)
-
-    def backward(chunk, carry):
+    square_copies = []
+    for i, other in enumerate([place.sibling(), place.other_y(), place.across()]):
+        copy = pltpu.make_async_remote_copy(
+            src_ref=square_ref,
+            dst_ref=square_buf.at[i],
+            send_sem=square_send.at[i],
+            recv_sem=square_recv.at[i],
+            device_id=other,
+            device_id_type=pl.DeviceIdType.MESH,
+        )
+        copy.start()
+        square_copies.append(copy)
+
+    scatter = Scatter(place, sums_ref, work, buffers, scatter_send, scatter_recv)
+
+    def divide(xf, j):
+        chunk = chunk_at(xf, j)
         span = pl.ds(pl.multiple_of(chunk * width, 64), width)
         parts = []
         for e in range(experts):
@@ -331,114 +413,66 @@
         sums_ref[pl.ds(chunk * d_count, d_count)] = total.astype(BF16).reshape(
             d_count, block_rows, width
         )
+        scatter.to_sibling(xf, j)
+
+    def far(j):
+        scatter.pass_on(1, 1, j)
+
+        @pl.when(place.k == 1)
+        def _():
+            scatter.pass_on(1, 0, j)
+
+    def near(j):
+        @pl.when(place.k == 0)
+        def _():
+            scatter.pass_on(1, 0, j)
+
+        scatter.pass_on(0, 1, j)
+
+    def backward_far(i, carry):
+        divide(1, (i + 1) % Z_COUNT)
+
+        @pl.when(i > 0)
+        def _():
+            far(i)
+
         return carry
 
-    lax.fori_loop(0, chunks, backward, 0)
-
-
-class Scatter:
-    def __init__(self, place, sums, work, buffers, send_sem, recv_sem):
-        self.place, self.sums, self.work = place, sums, work
-        self.buffers = buffers
-        self.send_sem, self.recv_sem = send_sem, recv_sem
-        self.sent = []
-
-    def copy(self, src, dst, device, send_index, recv_index):
-        return pltpu.make_async_remote_copy(
-            src_ref=src,
-            dst_ref=dst,
-            send_sem=self.send_sem.at[send_index],
-            recv_sem=self.recv_sem.at[recv_index],
-            device_id=device,
-            device_id_type=pl.DeviceIdType.MESH,
-        )
-
-    def send(self, src, slot, device):
-        copy = self.copy(src, self.buffers.at[slot], device, len(self.sent), slot)
-        copy.start()
-        self.sent.append(copy)
-
-    def take(self, slot):
-        place = self.place
-        landed = self.buffers.at[slot]
-        self.copy(landed, landed, place.sibling(), 0, slot).wait_recv()
-        return self.buffers[slot].astype(F32)
-
-    def to_sibling(self, s, f, j):
-        place = self.place
-        unit = place.unit(1 - place.k, s, f, j)
-        self.send(self.sums.at[unit], label(s, f, j), place.sibling())
-
-    def collect(self, s, f, j):
-        place = self.place
-        total = self.sums[place.unit(place.k, s, f, j)].astype(F32)
-        total = total + self.take(label(s, f, j))
-        if s == 0:
-            total = total + self.take(16 + f * 4 + j)
-        if s == 0 and f == 0:
-            total = total + self.take(24 + j)
-        return total
-
-    def pass_on(self, s, f, j):
-        place = self.place
-        held = label(s, f, j)
-        self.work[held] = self.collect(s, f, j).astype(BF16)
-        if s == 1:
-            self.send(self.work.at[held], 16 + f * 4 + j, place.second())
-        elif f == 1:
-            self.send(self.work.at[held], 24 + j, place.first())
-        else:
-            self.send(self.work.at[held], 27 + j, place.along_z(j))
-
-    def finish(self):
-        for copy in self.sent:
-            copy.wait_send()
-
-
-def scatter_kernel(
-    sums_ref, square_ref, token_ref, squares_ref,
-    work, buffers, square_buf, send_sem, recv_sem, square_send, square_recv,
-):
-    place = Place()
-    place.enter()
-    scatter = Scatter(place, sums_ref, work, buffers, send_sem, recv_sem)
-    others = [place.sibling(), place.other_y(), place.across()]
-    square_copies = []
-    for i, other in enumerate(others):
-        copy = pltpu.make_async_remote_copy(
-            src_ref=square_ref,
-            dst_ref=square_buf.at[i],
-            send_sem=square_send.at[i],
-            recv_sem=square_recv.at[i],
-            device_id=other,
-            device_id_type=pl.DeviceIdType.MESH,
-        )
-        copy.start()
-        square_copies.append(copy)
-    order = [(s, f) for s in (1, 0) for f in (1, 0)]
-    for s, f in order:
-        for j in (1, 2, 3, 0):
-            scatter.to_sibling(s, f, j)
-    for s, f in order:
-        for j in (1, 2, 3, 0):
-            if (s, f, j) != (0, 0, 0):
-                scatter.pass_on(s, f, j)
-    total = scatter.collect(0, 0, 0)
-    for j in range(1, Z_COUNT):
-        total = total + scatter.take(27 + j)
-    token_ref[...] = total.astype(BF16)
-    squares = square_ref[...]
+    def backward_near(i, carry):
+        divide(0, (i + 1) % Z_COUNT)
+
+        @pl.when(i > 0)
+        def _():
+            near(i)
+
+        @pl.when(i == 0)
+        def _():
+            far(0)
+
+        return carry
+
+    lax.fori_loop(0, Z_COUNT, backward_far, 0)
+    lax.fori_loop(0, Z_COUNT, backward_near, 0)
+    near(0)
+    total_squares = square_ref[...]
     for i, copy in enumerate(square_copies):
         copy.wait()
-        squares = squares + square_buf[i]
-    squares_ref[...] = squares
+        total_squares = total_squares + square_buf[i]
+    mean = total_squares / (2.0 * chunks * width * units * d_count)
+    scale = jnp.minimum(1.0, limit_ref[...] / jnp.sqrt(mean + 1e-06))
+    for e in range(experts):
+        scale_ref[e] = scale[e : e + 1]
+    for j in (1, 2, 3, 0):
+        total_ref[j] = scatter.collect(0, 0, j).astype(BF16)
+    gather.finish()
     scatter.finish()
 
 
-def weight_grad_kernel(count, scale_ref, rows_ref, act_ref, gate_ref, up_ref):
+def weight_grad_kernel(count, scale_ref, rows_ref, act_ref, hidden_ref, gate_ref, up_ref, out_ref):
     width = rows_ref.shape[2]
     units = gate_ref.shape[2]
-    scale = scale_ref[pl.program_id(0)]
+    scale = scale_ref[0, 0:1, 0:1]
+    out_ref[...] = hidden_ref[...]
     for chunk in range(count):
         raw = dot(rows_ref[chunk], act_ref[0], OVER_ROWS) * scale
         gate_ref[0, chunk * width : (chunk + 1) * width] = raw[:, :units].astype(BF16)
@@ -458,88 +492,81 @@
     slots = d_count * capacity
     all_units = chunks * d_count
     token_rows = d_count * block_rows
-    units = pl.pallas_call(
-        gather_kernel,
-        out_shape=jax.ShapeDtypeStruct((all_units, block_rows, width), BF16),
-        in_specs=whole_vmem(1),
-        out_specs=whole_vmem(1)[0],
-        scratch_shapes=[pltpu.SemaphoreType.DMA((31,)), pltpu.SemaphoreType.DMA((32,))],
-        compiler_params=pltpu.CompilerParams(
-            collective_id=0, has_side_effects=True, vmem_limit_bytes=VMEM_LIMIT
-        ),
-        name="gather_tokens",
-    )(tokens)
-    hidden, act, rows, sums, square = pl.pallas_call(
+    limit = jnp.broadcast_to(jnp.pad(clip_limit, (0, 8 - experts))[:, None], (8, 128))
+    dma = pltpu.SemaphoreType.DMA
+    hidden, act, rows, scale, totals = pl.pallas_call(
         expert_kernel,
         out_shape=[
             jax.ShapeDtypeStruct((experts, slots, hidden_units), BF16),
             jax.ShapeDtypeStruct((experts, slots, 2 * hidden_units), BF16),
             jax.ShapeDtypeStruct((chunks, experts * slots, width), BF16),
-            jax.ShapeDtypeStruct((all_units, block_rows, width), BF16),
-            jax.ShapeDtypeStruct((8, 128), F32),
+            jax.ShapeDtypeStruct((experts, 1, 128), F32),
+            jax.ShapeDtypeStruct((Z_COUNT, block_rows, width), BF16),
         ],
-        in_specs=whole_vmem(3) + [pl.BlockSpec(memory_space=pl.ANY)] * 2,
+        in_specs=whole_vmem(4) + [pl.BlockSpec(memory_space=pl.ANY)] * 2,
         out_specs=whole_vmem(5),
         scratch_shapes=[
+            pltpu.VMEM((all_units, block_rows, width), BF16),
+            pltpu.VMEM((all_units, block_rows, width), BF16),
             pltpu.VMEM((experts, model_width, hidden_units), BF16),
             pltpu.VMEM((experts, model_width, hidden_units), BF16),
             pltpu.VMEM((experts * slots, token_rows), BF16),
             pltpu.VMEM((experts, slots, 2 * hidden_units), F32),
             pltpu.VMEM((experts, slots, slots), F32),
             pltpu.VMEM((token_rows, experts * slots), BF16),
-            pltpu.SemaphoreType.DMA((2, chunks)),
-        ],
-        compiler_params=pltpu.CompilerParams(vmem_limit_bytes=VMEM_LIMIT),
-        name="experts",
-    )(routes.T, units, hidden_grad.reshape(experts, slots, hidden_units), gate_weight, up_weight)
-    token_grad, squares = pl.pallas_call(
-        scatter_kernel,
-        out_shape=[
-            jax.ShapeDtypeStruct((block_rows, width), BF16),
-            jax.ShapeDtypeStruct((8, 128), F32),
-        ],
-        in_specs=whole_vmem(2),
-        out_specs=whole_vmem(2),
-        scratch_shapes=[
             pltpu.VMEM((16, block_rows, width), BF16),
-            pltpu.VMEM((31, block_rows, width), BF16),
+            pltpu.VMEM((28, block_rows, width), BF16),
+            pltpu.VMEM((8, 128), F32),
             pltpu.VMEM((3, 8, 128), F32),
-            pltpu.SemaphoreType.DMA((31,)),
-            pltpu.SemaphoreType.DMA((31,)),
-            pltpu.SemaphoreType.DMA((3,)),
-            pltpu.SemaphoreType.DMA((3,)),
+            dma((2, chunks)), dma((31,)), dma((32,)), dma((28,)), dma((28,)), dma((3,)), dma((3,)),
         ],
         compiler_params=pltpu.CompilerParams(
-            collective_id=1, has_side_effects=True, vmem_limit_bytes=VMEM_LIMIT
+            collective_id=0, has_side_effects=True, vmem_limit_bytes=VMEM_LIMIT
         ),
-        name="scatter_grads",
-    )(sums, square)
-    grad_gate, grad_up = weight_grads(rows, act, squares, clip_limit, gate_weight.shape, d_count)
-    return (hidden.reshape(hidden_grad.shape), grad_gate, grad_up, token_grad)
-
-
-def weight_grads(rows, act, squares, clip_limit, shape, d_count):
+        name="experts",
+    )(
+        tokens, routes.T, hidden_grad.reshape(experts, slots, hidden_units), limit,
+        gate_weight, up_weight,
+    )
+    arrived = []
+    for j in range(1, Z_COUNT):
+        pairs = [(i, 2 * ((i // 2) ^ j) + i % 2) for i in range(chunks)]
+        arrived.append(lax.ppermute(totals[j], "expert", pairs))
+    grad_gate, grad_up, hidden = weight_grads(rows, act, hidden, scale, gate_weight.shape)
+    token_grad = totals[0].astype(F32)
+    for block in arrived:
+        token_grad = token_grad + block.astype(F32)
+    return (hidden.reshape(hidden_grad.shape), grad_gate, grad_up, token_grad.astype(BF16))
+
+
+def weight_grads(rows, act, hidden, scale, shape):
     experts, model_width, hidden_units = shape
     chunks, _, width = rows.shape
     slots = act.shape[1]
-    mean = squares[:experts, 0] / (2.0 * model_width * hidden_units * d_count)
-    scale = jnp.minimum(1.0, clip_limit / jnp.sqrt(mean + 1e-06))
     halves = 2
     count = chunks // halves
     out_block = pl.BlockSpec((1, count * width, hidden_units), lambda e, h: (e, h, 0))
+    hidden_block = pl.BlockSpec((1, slots, hidden_units), lambda e, h: (e, 0, 0))
     return pl.pallas_call(
         functools.partial(weight_grad_kernel, count),
         grid=(experts, halves),
-        out_shape=[jax.ShapeDtypeStruct(shape, BF16)] * 2,
+        out_shape=[jax.ShapeDtypeStruct(shape, BF16)] * 2
+        + [jax.ShapeDtypeStruct(hidden.shape, BF16)],
         in_specs=[
-            pl.BlockSpec(memory_space=pltpu.SMEM),
+            pl.BlockSpec((1, 1, 128), lambda e, h: (e, 0, 0)),
             pl.BlockSpec((count, slots, width), lambda e, h: (h, e, 0)),
             pl.BlockSpec((1, slots, 2 * hidden_units), lambda e, h: (e, 0, 0)),
+            hidden_block,
         ],
-        out_specs=[out_block, out_block],
+        out_specs=[out_block, out_block, hidden_block],
+        cost_estimate=pl.CostEstimate(
+            flops=4 * experts * slots * model_width * hidden_units,
+            bytes_accessed=4 * experts * model_width * hidden_units + 2 * rows.size,
+            transcendentals=0,
+        ),
         compiler_params=pltpu.CompilerParams(vmem_limit_bytes=VMEM_LIMIT),
         name="weight_grads",
-    )(scale, rows, act)
+    )(scale, rows, act, hidden)
 
 
 def solution(mesh):

time: 103 us -> 82.4 us (0.80)
  Pallas kernels: 99.5 us -> 73.7 us
  starting transfers between devices: 0 us -> 3.55 us
    pallas_call x2 -> x0, Pallas kernels: 57.3 us -> none  [the longest x1 31 us: kernel_body(): pl.pallas_call(gather_kernel, out_shape=jax.ShapeDtypeStruct((all_units,...]
    pallas_call x1, Pallas kernels: 28.3 us -> 59.5 us  [kernel_body(): pl.pallas_call(expert_kernel, out_shape=[jax.ShapeDtypeStruct((experts, s...]
    ppermute x0 -> x3, starting transfers between devices: none -> 3.55 us  [kernel_body(): arrived.append(lax.ppermute(totals[j], 'expert', pairs))]
    convert_element_type x0 -> x1, other arithmetic: none -> 1.59 us  [kernel_body(): token_grad.astype(BF16)]
    unnamed x3 -> x0, local copies, waits for them, and re-layouts: 1.54 us -> none
  transfers between devices with their start and end apart: 0 -> 3, of which waited for: 0 -> 0; matrix products, arithmetic and copies ran while one was open for 0% -> 0% of each run, Pallas kernels for 0% -> 17%
where the time goes in v2:
time: 82.4 us; the launch traced here: 81.9 us
  Pallas kernels  73.7 us (89%)
  starting transfers between devices  3.55 us (4%)
  local copies, waits for them, and re-layouts  2.33 us (3%)
  other arithmetic  1.59 us (2%)
    pallas_call x1, Pallas kernels, kernel_body(): pl.pallas_call(expert_kernel, out_shape=[jax.ShapeDtypeStruct((experts, s...  59.5 us
    pallas_call x1, Pallas kernels, weight_grads(): pl.pallas_call(functools.partial(weight_grad_kernel, count), grid=(expert...  14.2 us
    ppermute x3, starting transfers between devices, kernel_body(): arrived.append(lax.ppermute(totals[j], 'expert', pairs))  3.55 us
  transfers between devices with their start and end apart: 3, of which 0 were waited for; matrix products, arithmetic and copies ran while one was open for 0% of the time, Pallas kernels for 17%

profile of v2, /device:TPU:0, one launch (start us, length us, event | category | flops | bytes accessed | tf_op | source)
XLA Modules:
  0.0 81.9 jit_solution(15187798323367739319)
XLA Ops:
  0.6 0.7 pad.4
  1.3 0.7 broadcast_in_dim.2.limit_ref
  2.0 59.5 %experts.1 = (bf16[4,128,512]{2,1,0:T(8,128)(2,1)}, bf16[4,128,1024]{2,1,0:T(8,128)(2,1)}, bf16[8,512,448]{2,1,0:T(8,128)(2,1)}, f32[4,1,128]{2,1,0:T(1,128)}, bf16[4,96,448]{2,1,0:T(8,128)(2,1)}) custom-call(bf16[96,448]{1,0:T(8,128)(2,1)} %tokens_ref.1, s32[8,384]{1,0:T(8,128)} %bitcast.13, bf16[4,128,512]{2,1,0:T(8,128)(2,1)} %bitcast.12, ...), custom_call_target="tpu_custom_call" | custom-call | tf_op jit(solution)/shard_map/experts/pallas_call | solution.py:497
  61.5 1.0 %slice_bitcast_fusion.2 = (bf16[96,448]{1,0:T(8,128)(2,1)S(1)}, bf16[96,448]{1,0:T(8,128)(2,1)S(1)}, bf16[96,448]{1,0:T(8,128)(2,1)S(1)}) fusion(bf16[4,96,448]{2,1,0:T(8,128)(2,1)} %get-tuple-element.19), kind=kLoop, calls=%fused_computation.6 | loop fusion | bytes 516096 | tf_op jit(solution)/shard_map/squeeze | solution.py:534
  62.5 1.1 %collective-permute-start = (bf16[96,448]{1,0:T(8,128)(2,1)S(1)}, bf16[96,448]{1,0:T(8,128)(2,1)S(1)}, u32[]{:S(2)}, u32[]{:S(2)}) collective-permute-start(bf16[96,448]{1,0:T(8,128)(2,1)S(1)} %get-tuple-element.20), channel_id=1, source_target_pairs={{0,2},{1,3},{2,0},{3,1},{4,6},{5,7},{6,4},{7,5},{8,10},{9,11},{10,... | collective-permute-start | bytes 258056 | tf_op jit(solution)/shard_map/ppermute | solution.py:534
  63.6 0.3 collective-permute-start.2
  63.9 2.1 %collective-permute-start.1 = (bf16[96,448]{1,0:T(8,128)(2,1)S(1)}, bf16[96,448]{1,0:T(8,128)(2,1)S(1)}, u32[]{:S(2)}, u32[]{:S(2)}) collective-permute-start(bf16[96,448]{1,0:T(8,128)(2,1)S(1)} %get-tuple-element.22), channel_id=1, source_target_pairs={{0,4},{1,5},{2,6},{3,7},{4,0},{5,1},{6,2},{7,3},{8,12},{9,13},{10,... | collective-permute-start | bytes 258056 | tf_op jit(solution)/shard_map/ppermute | solution.py:534
  66.0 14.2 %weight_grads.1 = (bf16[4,3584,512]{2,1,0:T(8,128)(2,1)}, bf16[4,3584,512]{2,1,0:T(8,128)(2,1)}, bf16[4,128,512]{2,1,0:T(8,128)(2,1)}) custom-call(f32[4,1,128]{2,1,0:T(1,128)} %get-tuple-element.12.scale_ref, bf16[8,512,448]{2,1,0:T(8,128)(2,1)} %get-tuple-element.13.rows_ref, bf16[4,128,1024]{2,1,0:T(8,128)(2,1)} %get-tuple-element.14.act_ref, ...), custom_call_target="tpu_custom_call" | custom-call | flops 3758096384 | bytes 33030144 | tf_op jit(solution)/shard_map/weight_grads/pallas_call | solution.py:550
  80.3 0.0 collective-permute-done
  80.3 0.0 collective-permute-done.2
  80.3 0.0 collective-permute-done.1
  80.3 1.6 %fusion.2 = bf16[96,448]{1,0:T(8,128)(2,1)} fusion(bf16[96,448]{1,0:T(8,128)(2,1)S(1)} %collective-permute-done.2, bf16[96,448]{1,0:T(8,128)(2,1)S(1)} %collective-permute-done.1, bf16[96,448]{1,0:T(8,128)(2,1)S(1)} %collective-permute-done, bf16[4,96,448]{2,1,0:T(8,128)(2,1)} %get-tuple-element.19), kind=kLoop, calls=%fused_computation.3 | loop fusion | flops 344064 | bytes 430080 | tf_op jit(solution)/shard_map/convert_element_type | solution.py:539
Async XLA Ops:
  62.5 17.8 %collective-permute-start = (bf16[96,448]{1,0:T(8,128)(2,1)S(1)}, bf16[96,448]{1,0:T(8,128)(2,1)S(1)}, u32[]{:S(2)}, u32[]{:S(2)}) collective-permute-start(bf16[96,448]{1,0:T(8,128)(2,1)S(1)} %get-tuple-element.20), channel_id=1, source_target_pairs={{0,2},{1,3},{2,0},{3,1},{4,6},{5,7},{6,4},{7,5},{8,10},{9,11},{10,... | collective-permute-start | bytes 258056 | tf_op jit(solution)/shard_map/ppermute | solution.py:534
  63.6 16.7 %collective-permute-start.2 = (bf16[96,448]{1,0:T(8,128)(2,1)S(1)}, bf16[96,448]{1,0:T(8,128)(2,1)S(1)}, u32[]{:S(2)}, u32[]{:S(2)}) collective-permute-start(bf16[96,448]{1,0:T(8,128)(2,1)S(1)} %get-tuple-element.21), channel_id=1, source_target_pairs={{0,6},{1,7},{2,4},{3,5},{4,2},{5,3},{6,0},{7,1},{8,14},{9,15},{10,... | collective-permute-start | bytes 258056 | tf_op jit(solution)/shard_map/ppermute | solution.py:534
  63.9 16.4 %collective-permute-start.1 = (bf16[96,448]{1,0:T(8,128)(2,1)S(1)}, bf16[96,448]{1,0:T(8,128)(2,1)S(1)}, u32[]{:S(2)}, u32[]{:S(2)}) collective-permute-start(bf16[96,448]{1,0:T(8,128)(2,1)S(1)} %get-tuple-element.22), channel_id=1, source_target_pairs={{0,4},{1,5},{2,6},{3,7},{4,0},{5,1},{6,2},{7,3},{8,12},{9,13},{10,... | collective-permute-start | bytes 258056 | tf_op jit(solution)/shard_map/ppermute | solution.py:534

commit v3 on v2

--- a/solution.py
+++ b/solution.py
@@ -142,15 +142,19 @@
     def other_y(self):
         return (2 * (1 - self.y) + self.k, self.ex)
 
-    def enter(self):
+    def partners(self):
+        others = [self.sibling(), self.first(), self.second(), self.across()]
+        return others + [self.along_z(j) for j in range(1, Z_COUNT)]
+
+    def greet(self):
         barrier = pltpu.get_barrier_semaphore()
-        partners = [self.sibling(), self.first(), self.second(), self.across()]
-        partners += [self.along_z(j) for j in range(1, Z_COUNT)]
-        for partner in partners:
+        for partner in self.partners():
             pl.semaphore_signal(
                 barrier, inc=1, device_id=partner, device_id_type=pl.DeviceIdType.MESH
             )
-        pl.semaphore_wait(barrier, len(partners))
+
+    def enter(self):
+        pl.semaphore_wait(pltpu.get_barrier_semaphore(), len(self.partners()))
 
 
 def label(s, f, j):
@@ -200,10 +204,8 @@
             self.copy(self.place.unit(self.place.k, 0, 0, 0), self.place.sibling(), i, 0).wait_send()
 
 
-def one_hot_rows(routes_ref, first_expert, experts, capacity, block_rows):
-    tokens = routes_ref.shape[1]
-    blocks = tokens // block_rows
-    routes = routes_ref[...]
+def one_hot_rows(routes, first_expert, experts, capacity):
+    tokens = routes.shape[1]
     masks = [
         jnp.sum((routes == first_expert + e).astype(F32), axis=0, keepdims=True)
         for e in range(experts)
@@ -211,16 +213,10 @@
     mask = jnp.concatenate(masks + [jnp.zeros((8 - experts, tokens), F32)], axis=0)
     earlier = lax.broadcasted_iota(jnp.int32, (tokens, tokens), 0)
     later = lax.broadcasted_iota(jnp.int32, (tokens, tokens), 1)
-    block_start = jnp.zeros((tokens, tokens), jnp.int32)
-    slot_start = jnp.zeros((8, tokens), jnp.int32)
-    token = lax.broadcasted_iota(jnp.int32, (8, tokens), 1)
-    for b in range(1, blocks):
-        block_start = jnp.where(later >= b * block_rows, b * block_rows, block_start)
-        slot_start = jnp.where(token >= b * block_rows, b * capacity, slot_start)
-    counted = jnp.where((earlier < later) & (earlier >= block_start), 1.0, 0.0).astype(BF16)
+    counted = jnp.where(earlier < later, 1.0, 0.0).astype(BF16)
     rank = jnp.dot(mask.astype(BF16), counted, preferred_element_type=F32)
-    slot = jnp.where(mask > 0.5, rank + slot_start.astype(F32), -1.0)
-    rows = lax.broadcasted_iota(jnp.int32, (blocks * capacity, tokens), 0).astype(F32)
+    slot = jnp.where(mask > 0.5, rank, -1.0)
+    rows = lax.broadcasted_iota(jnp.int32, (capacity, tokens), 0).astype(F32)
     return jnp.concatenate(
         [jnp.where(rows == slot[e : e + 1], 1.0, 0.0).astype(BF16) for e in range(experts)], axis=0
     )
@@ -309,7 +305,7 @@
 
 def expert_kernel(
     tokens_ref, routes_ref, grad_ref, limit_ref, gate_hbm, up_hbm,
-    hidden_ref, act_ref, rows_ref, scale_ref, total_ref,
+    hidden_ref, act_ref, rows_ref, scale_ref, total_0, total_1, total_2, total_3,
     units_ref, sums_ref, gate_v, up_v, onehot_ref, acc_ref, gram_ref, back_ref,
     work, buffers, square_ref, square_buf,
     weight_sem, gather_send, gather_recv, scatter_send, scatter_recv, square_send, square_recv,
@@ -318,9 +314,9 @@
     chunks = rows_ref.shape[0]
     width = rows_ref.shape[2]
     d_count = units_ref.shape[0] // chunks
-    block_rows = units_ref.shape[1]
-    tokens = d_count * block_rows
+    block_rows = tokens_ref.shape[0]
     place = Place()
+    total_refs = (total_0, total_1, total_2, total_3)
 
     def chunk_at(xf, j):
         return 2 * place.z_at(j) + flip(place.x, xf)
@@ -332,23 +328,27 @@
         for xf in range(2):
             for copy in weights(chunk_at(xf, j)):
                 copy.start()
+    place.greet()
     units_ref[place.unit(place.k, 0, 0, 0)] = tokens_ref[...]
+    capacity = slots // d_count
+    first_expert = place.ex * experts
+    onehots = []
+    for d in range(d_count):
+        routes = routes_ref[:, d * block_rows : (d + 1) * block_rows]
+        onehots.append(one_hot_rows(routes, first_expert, experts, capacity))
+        onehot_ref[d] = onehots[d]
     place.enter()
     gather = Gather(place, units_ref, gather_send, gather_recv)
     gather.forward(0, 0, 0, own=True)
-
-    first_expert = place.ex * experts
-    onehot = one_hot_rows(routes_ref, first_expert, experts, slots // d_count, block_rows)
-    onehot_ref[...] = onehot
-    back_ref[...] = onehot.T
+    for d in range(d_count):
+        back_ref[d] = onehots[d].T
     acc_ref[...] = jnp.zeros_like(acc_ref)
     gram_ref[...] = jnp.zeros_like(gram_ref)
-
-    for j in range(Z_COUNT):
-        if j > 0:
-            gather.forward(0, 0, j)
-        gather.forward(0, 1, j)
+    gather.forward(0, 1, 0)
+    gather.forward(0, 0, 1)
     gather.forward(1, 0, 0)
+    gather.forward(0, 1, 1)
+    gather.forward(0, 0, 2)
     gather.forward(1, 1, 0)
 
     def multiply(xf, j):
@@ -357,8 +357,11 @@
         gather.from_sibling(xf, 1, j)
         for copy in weights(chunk):
             copy.wait()
-        here = units_ref[pl.ds(chunk * d_count, d_count)].reshape(tokens, width)
-        rows_ref[chunk] = dot(onehot_ref[...], here).astype(BF16)
+        for d in range(d_count):
+            found = dot(onehot_ref[d], units_ref[chunk * d_count + d]).astype(BF16)
+            for e in range(experts):
+                at = e * slots + d * capacity
+                rows_ref[chunk, at : at + capacity] = found[e * capacity : (e + 1) * capacity]
         span = pl.ds(pl.multiple_of(chunk * width, 64), width)
         for e in range(experts):
             mine = rows_ref[chunk, e * slots : (e + 1) * slots]
@@ -368,6 +371,14 @@
 
     def forward(j, carry):
         multiply(0, j)
+
+        @pl.when(j == 0)
+        def _():
+            gather.forward(0, 0, 3)
+
+        @pl.when(j < Z_COUNT - 2)
+        def _():
+            gather.forward(0, 1, j + 2)
 
         @pl.when(j < Z_COUNT - 1)
         def _():
@@ -409,10 +420,10 @@
             part = dot(act_ref[e, :, :units], gate_v[e, span], OVER_LANES)
             part = part + dot(act_ref[e, :, units:], up_v[e, span], OVER_LANES)
             parts.append(part.astype(BF16))
-        total = dot(back_ref[...], jnp.concatenate(parts, axis=0))
-        sums_ref[pl.ds(chunk * d_count, d_count)] = total.astype(BF16).reshape(
-            d_count, block_rows, width
-        )
+        for d in range(d_count):
+            mine = [part[d * capacity : (d + 1) * capacity] for part in parts]
+            total = dot(back_ref[d], jnp.concatenate(mine, axis=0))
+            sums_ref[chunk * d_count + d] = total.astype(BF16)
         scatter.to_sibling(xf, j)
 
     def far(j):
@@ -459,11 +470,11 @@
         copy.wait()
         total_squares = total_squares + square_buf[i]
     mean = total_squares / (2.0 * chunks * width * units * d_count)
-    scale = jnp.minimum(1.0, limit_ref[...] / jnp.sqrt(mean + 1e-06))
+    root_mean = jnp.sqrt(mean + 1e-06)
     for e in range(experts):
-        scale_ref[e] = scale[e : e + 1]
+        scale_ref[e] = jnp.minimum(1.0, limit_ref[e] / root_mean[e : e + 1])
     for j in (1, 2, 3, 0):
-        total_ref[j] = scatter.collect(0, 0, j).astype(BF16)
+        total_refs[j][...] = scatter.collect(0, 0, j).astype(BF16)
     gather.finish()
     scatter.finish()
 
@@ -474,9 +485,11 @@
     scale = scale_ref[0, 0:1, 0:1]
     out_ref[...] = hidden_ref[...]
     for chunk in range(count):
-        raw = dot(rows_ref[chunk], act_ref[0], OVER_ROWS) * scale
-        gate_ref[0, chunk * width : (chunk + 1) * width] = raw[:, :units].astype(BF16)
-        up_ref[0, chunk * width : (chunk + 1) * width] = raw[:, units:].astype(BF16)
+        turned = rows_ref[chunk].T
+        for start in range(0, 2 * units, 256):
+            raw = dot(turned, act_ref[0, :, start : start + 256]) * scale
+            out, at = (gate_ref, start) if start < units else (up_ref, start - units)
+            out[0, chunk * width : (chunk + 1) * width, at : at + 256] = raw.astype(BF16)
 
 
 def whole_vmem(count):
@@ -491,29 +504,29 @@
     capacity = hidden_grad.shape[2]
     slots = d_count * capacity
     all_units = chunks * d_count
-    token_rows = d_count * block_rows
-    limit = jnp.broadcast_to(jnp.pad(clip_limit, (0, 8 - experts))[:, None], (8, 128))
     dma = pltpu.SemaphoreType.DMA
-    hidden, act, rows, scale, totals = pl.pallas_call(
+    hidden, act, rows, scale, *totals = pl.pallas_call(
         expert_kernel,
         out_shape=[
             jax.ShapeDtypeStruct((experts, slots, hidden_units), BF16),
             jax.ShapeDtypeStruct((experts, slots, 2 * hidden_units), BF16),
             jax.ShapeDtypeStruct((chunks, experts * slots, width), BF16),
             jax.ShapeDtypeStruct((experts, 1, 128), F32),
-            jax.ShapeDtypeStruct((Z_COUNT, block_rows, width), BF16),
-        ],
-        in_specs=whole_vmem(4) + [pl.BlockSpec(memory_space=pl.ANY)] * 2,
-        out_specs=whole_vmem(5),
+        ]
+        + [jax.ShapeDtypeStruct((block_rows, width), BF16)] * Z_COUNT,
+        in_specs=whole_vmem(3)
+        + [pl.BlockSpec(memory_space=pltpu.SMEM)]
+        + [pl.BlockSpec(memory_space=pl.ANY)] * 2,
+        out_specs=whole_vmem(4 + Z_COUNT),
         scratch_shapes=[
             pltpu.VMEM((all_units, block_rows, width), BF16),
             pltpu.VMEM((all_units, block_rows, width), BF16),
             pltpu.VMEM((experts, model_width, hidden_units), BF16),
             pltpu.VMEM((experts, model_width, hidden_units), BF16),
-            pltpu.VMEM((experts * slots, token_rows), BF16),
+            pltpu.VMEM((d_count, experts * capacity, block_rows), BF16),
             pltpu.VMEM((experts, slots, 2 * hidden_units), F32),
             pltpu.VMEM((experts, slots, slots), F32),
-            pltpu.VMEM((token_rows, experts * slots), BF16),
+            pltpu.VMEM((d_count, block_rows, experts * capacity), BF16),
             pltpu.VMEM((16, block_rows, width), BF16),
             pltpu.VMEM((28, block_rows, width), BF16),
             pltpu.VMEM((8, 128), F32),
@@ -525,7 +538,7 @@
         ),
         name="experts",
     )(
-        tokens, routes.T, hidden_grad.reshape(experts, slots, hidden_units), limit,
+        tokens, routes.T, hidden_grad.reshape(experts, slots, hidden_units), clip_limit,
         gate_weight, up_weight,
     )
     arrived = []

time: 82.4 us -> 75.6 us (0.917)
  Pallas kernels: 73.7 us -> 68.4 us
  local copies, waits for them, and re-layouts: 2.33 us -> 0 us
  starting transfers between devices: 3.55 us -> 4.45 us
    pallas_call x1, Pallas kernels: 59.5 us -> 54.2 us  [kernel_body(): pl.pallas_call(expert_kernel, out_shape=[jax.ShapeDtypeStruct((experts, s...]
    squeeze x1 -> x0, local copies, waits for them, and re-layouts: 1.01 us -> none  [kernel_body(): arrived.append(lax.ppermute(totals[j], 'expert', pairs))]
    ppermute x3, starting transfers between devices: 3.55 us -> 4.45 us  [kernel_body(): arrived.append(lax.ppermute(totals[j], 'expert', pairs))]
  transfers between devices with their start and end apart: 3 -> 3, of which waited for: 0 -> 0; matrix products, arithmetic and copies ran while one was open for 0% -> 0% of each run, Pallas kernels for 17% -> 19%
where the time goes in v3:
time: 75.6 us; the launch traced here: 75.1 us
  Pallas kernels  68.4 us (90%)
  starting transfers between devices  4.45 us (6%)
  other arithmetic  1.59 us (2%)
    pallas_call x1, Pallas kernels, kernel_body(): pl.pallas_call(expert_kernel, out_shape=[jax.ShapeDtypeStruct((experts, s...  54.2 us
    pallas_call x1, Pallas kernels, weight_grads(): pl.pallas_call(functools.partial(weight_grad_kernel, count), grid=(expert...  14.2 us
    ppermute x3, starting transfers between devices, kernel_body(): arrived.append(lax.ppermute(totals[j], 'expert', pairs))  4.45 us
    convert_element_type x1, other arithmetic, kernel_body(): token_grad.astype(BF16)  1.59 us
  transfers between devices with their start and end apart: 3, of which 0 were waited for; matrix products, arithmetic and copies ran while one was open for 0% of the time, Pallas kernels for 19%

profile of v3, /device:TPU:0, one launch (start us, length us, event | category | flops | bytes accessed | tf_op | source)
XLA Modules:
  0.0 75.1 jit_solution(10547449942736496794)
XLA Ops:
  0.6 54.2 %experts.1 = (bf16[4,128,512]{2,1,0:T(8,128)(2,1)}, bf16[4,128,1024]{2,1,0:T(8,128)(2,1)}, bf16[8,512,448]{2,1,0:T(8,128)(2,1)}, f32[4,1,128]{2,1,0:T(1,128)}, b...) custom-call(bf16[96,448]{1,0:T(8,128)(2,1)} %tokens_ref.1, ...), custom_call_target="tpu_custom_call" | custom-call | tf_op jit(solution)/shard_map/experts/pallas_call | solution.py:508
  54.9 0.6 collective-permute-start
  55.4 1.4 %collective-permute-start.1 = (bf16[96,448]{1,0:T(8,128)(2,1)}, bf16[96,448]{1,0:T(8,128)(2,1)S(1)}, u32[]{:S(2)}, u32[]{:S(2)}) collective-permute-start(bf16[96,448]{1,0:T(8,128)(2,1)} %get-tuple-element.24), channel_id=1, source_target_pairs={{0,4},{1,5},{2,6},{3,7},{4,0},{5,1},{6,2},{7,3},{8,12},{9,13},{10,... | collective-permute-start | bytes 258056 | tf_op jit(solution)/shard_map/ppermute | solution.py:547
  56.8 2.5 %collective-permute-start.2 = (bf16[96,448]{1,0:T(8,128)(2,1)}, bf16[96,448]{1,0:T(8,128)(2,1)S(1)}, u32[]{:S(2)}, u32[]{:S(2)}) collective-permute-start(bf16[96,448]{1,0:T(8,128)(2,1)} %get-tuple-element.25), channel_id=1, source_target_pairs={{0,6},{1,7},{2,4},{3,5},{4,2},{5,3},{6,0},{7,1},{8,14},{9,15},{10,... | collective-permute-start | bytes 258056 | tf_op jit(solution)/shard_map/ppermute | solution.py:547
  59.3 14.2 %weight_grads.1 = (bf16[4,3584,512]{2,1,0:T(8,128)(2,1)}, bf16[4,3584,512]{2,1,0:T(8,128)(2,1)}, bf16[4,128,512]{2,1,0:T(8,128)(2,1)}) custom-call(f32[4,1,128]{2,1,0:T(1,128)} %get-tuple-element.15.scale_ref, bf16[8,512,448]{2,1,0:T(8,128)(2,1)} %get-tuple-element.16.rows_ref, bf16[4,128,1024]{2,1,0:T(8,128)(2,1)} %get-tuple-element.17.act_ref, ...), custom_call_target="tpu_custom_call" | custom-call | flops 3758096384 | bytes 33030144 | tf_op jit(solution)/shard_map/weight_grads/pallas_call | solution.py:563
  73.5 0.0 collective-permute-done
  73.5 0.0 collective-permute-done.1
  73.5 0.0 collective-permute-done.2
  73.6 1.6 %add_convert_fusion = bf16[96,448]{1,0:T(8,128)(2,1)} fusion(bf16[96,448]{1,0:T(8,128)(2,1)S(1)} %collective-permute-done.2, bf16[96,448]{1,0:T(8,128)(2,1)S(1)} %collective-permute-done.1, bf16[96,448]{1,0:T(8,128)(2,1)S(1)} %collective-permute-done, bf16[96,448]{1,0:T(8,128)(2,1)} %get-tuple-element.22), kind=kLoop, calls=%fused_computation | loop fusion | flops 344064 | bytes 430080 | tf_op jit(solution)/shard_map/convert_element_type | solution.py:552
Async XLA Ops:
  54.9 18.7 %collective-permute-start = (bf16[96,448]{1,0:T(8,128)(2,1)}, bf16[96,448]{1,0:T(8,128)(2,1)S(1)}, u32[]{:S(2)}, u32[]{:S(2)}) collective-permute-start(bf16[96,448]{1,0:T(8,128)(2,1)} %get-tuple-element.23), channel_id=1, source_target_pairs={{0,2},{1,3},{2,0},{3,1},{4,6},{5,7},{6,4},{7,5},{8,10},{9,11},{10,... | collective-permute-start | bytes 258056 | tf_op jit(solution)/shard_map/ppermute | solution.py:547
  55.4 18.1 %collective-permute-start.1 = (bf16[96,448]{1,0:T(8,128)(2,1)}, bf16[96,448]{1,0:T(8,128)(2,1)S(1)}, u32[]{:S(2)}, u32[]{:S(2)}) collective-permute-start(bf16[96,448]{1,0:T(8,128)(2,1)} %get-tuple-element.24), channel_id=1, source_target_pairs={{0,4},{1,5},{2,6},{3,7},{4,0},{5,1},{6,2},{7,3},{8,12},{9,13},{10,... | collective-permute-start | bytes 258056 | tf_op jit(solution)/shard_map/ppermute | solution.py:547
  56.8 16.7 %collective-permute-start.2 = (bf16[96,448]{1,0:T(8,128)(2,1)}, bf16[96,448]{1,0:T(8,128)(2,1)S(1)}, u32[]{:S(2)}, u32[]{:S(2)}) collective-permute-start(bf16[96,448]{1,0:T(8,128)(2,1)} %get-tuple-element.25), channel_id=1, source_target_pairs={{0,6},{1,7},{2,4},{3,5},{4,2},{5,3},{6,0},{7,1},{8,14},{9,15},{10,... | collective-permute-start | bytes 258056 | tf_op jit(solution)/shard_map/ppermute | solution.py:547

commit v4 on v3

--- a/solution.py
+++ b/solution.py
@@ -295,17 +295,19 @@
         self.work[held] = self.collect(s, f, j).astype(BF16)
         if s == 1:
             self.copy(self.work.at[held], 16 + f * 4 + j, place.second()).start()
+        elif f == 1:
+            self.copy(self.work.at[held], 24 + j, place.first()).start()
         else:
-            self.copy(self.work.at[held], 24 + j, place.first()).start()
+            self.copy(self.work.at[held], 27 + j, place.along_z(j)).start()
 
     def finish(self):
-        for slot in range(28):
+        for slot in range(31):
             self.copy(self.buffers.at[slot], slot, self.place.sibling()).wait_send()
 
 
 def expert_kernel(
     tokens_ref, routes_ref, grad_ref, limit_ref, gate_hbm, up_hbm,
-    hidden_ref, act_ref, rows_ref, scale_ref, total_0, total_1, total_2, total_3,
+    hidden_ref, act_ref, rows_ref, scale_ref, token_ref,
     units_ref, sums_ref, gate_v, up_v, onehot_ref, acc_ref, gram_ref, back_ref,
     work, buffers, square_ref, square_buf,
     weight_sem, gather_send, gather_recv, scatter_send, scatter_recv, square_send, square_recv,
@@ -316,7 +318,6 @@
     d_count = units_ref.shape[0] // chunks
     block_rows = tokens_ref.shape[0]
     place = Place()
-    total_refs = (total_0, total_1, total_2, total_3)
 
     def chunk_at(xf, j):
         return 2 * place.z_at(j) + flip(place.x, xf)
@@ -465,6 +466,8 @@
     lax.fori_loop(0, Z_COUNT, backward_far, 0)
     lax.fori_loop(0, Z_COUNT, backward_near, 0)
     near(0)
+    for j in range(1, Z_COUNT):
+        scatter.pass_on(0, 0, j)
     total_squares = square_ref[...]
     for i, copy in enumerate(square_copies):
         copy.wait()
@@ -473,17 +476,23 @@
     root_mean = jnp.sqrt(mean + 1e-06)
     for e in range(experts):
         scale_ref[e] = jnp.minimum(1.0, limit_ref[e] / root_mean[e : e + 1])
-    for j in (1, 2, 3, 0):
-        total_refs[j][...] = scatter.collect(0, 0, j).astype(BF16)
+    total = scatter.collect(0, 0, 0)
+    for j in range(1, Z_COUNT):
+        total = total + scatter.take(27 + j)
+    token_ref[...] = total.astype(BF16)
     gather.finish()
     scatter.finish()
 
 
-def weight_grad_kernel(count, scale_ref, rows_ref, act_ref, hidden_ref, gate_ref, up_ref, out_ref):
+def weight_grad_kernel(
+    count, scale_ref, rows_ref, act_ref, hidden_ref, token_ref,
+    gate_ref, up_ref, hidden_out, token_out,
+):
     width = rows_ref.shape[2]
     units = gate_ref.shape[2]
     scale = scale_ref[0, 0:1, 0:1]
-    out_ref[...] = hidden_ref[...]
+    hidden_out[...] = hidden_ref[...]
+    token_out[...] = token_ref[...]
     for chunk in range(count):
         turned = rows_ref[chunk].T
         for start in range(0, 2 * units, 256):
@@ -505,19 +514,19 @@
     slots = d_count * capacity
     all_units = chunks * d_count
     dma = pltpu.SemaphoreType.DMA
-    hidden, act, rows, scale, *totals = pl.pallas_call(
+    hidden, act, rows, scale, token_grad = pl.pallas_call(
         expert_kernel,
         out_shape=[
             jax.ShapeDtypeStruct((experts, slots, hidden_units), BF16),
             jax.ShapeDtypeStruct((experts, slots, 2 * hidden_units), BF16),
             jax.ShapeDtypeStruct((chunks, experts * slots, width), BF16),
             jax.ShapeDtypeStruct((experts, 1, 128), F32),
-        ]
-        + [jax.ShapeDtypeStruct((block_rows, width), BF16)] * Z_COUNT,
+            jax.ShapeDtypeStruct((block_rows, width), BF16),
+        ],
         in_specs=whole_vmem(3)
         + [pl.BlockSpec(memory_space=pltpu.SMEM)]
         + [pl.BlockSpec(memory_space=pl.ANY)] * 2,
-        out_specs=whole_vmem(4 + Z_COUNT),
+        out_specs=whole_vmem(5),
         scratch_shapes=[
             pltpu.VMEM((all_units, block_rows, width), BF16),
             pltpu.VMEM((all_units, block_rows, width), BF16),
@@ -528,10 +537,10 @@
             pltpu.VMEM((experts, slots, slots), F32),
             pltpu.VMEM((d_count, block_rows, experts * capacity), BF16),
             pltpu.VMEM((16, block_rows, width), BF16),
-            pltpu.VMEM((28, block_rows, width), BF16),
+            pltpu.VMEM((31, block_rows, width), BF16),
             pltpu.VMEM((8, 128), F32),
             pltpu.VMEM((3, 8, 128), F32),
-            dma((2, chunks)), dma((31,)), dma((32,)), dma((28,)), dma((28,)), dma((3,)), dma((3,)),
+            dma((2, chunks)), dma((31,)), dma((32,)), dma((31,)), dma((31,)), dma((3,)), dma((3,)),
         ],
         compiler_params=pltpu.CompilerParams(
             collective_id=0, has_side_effects=True, vmem_limit_bytes=VMEM_LIMIT
@@ -541,37 +550,34 @@
         tokens, routes.T, hidden_grad.reshape(experts, slots, hidden_units), clip_limit,
         gate_weight, up_weight,
     )
-    arrived = []
-    for j in range(1, Z_COUNT):
-        pairs = [(i, 2 * ((i // 2) ^ j) + i % 2) for i in range(chunks)]
-        arrived.append(lax.ppermute(totals[j], "expert", pairs))
-    grad_gate, grad_up, hidden = weight_grads(rows, act, hidden, scale, gate_weight.shape)
-    token_grad = totals[0].astype(F32)
-    for block in arrived:
-        token_grad = token_grad + block.astype(F32)
-    return (hidden.reshape(hidden_grad.shape), grad_gate, grad_up, token_grad.astype(BF16))
-
-
-def weight_grads(rows, act, hidden, scale, shape):
+    grad_gate, grad_up, hidden, token_grad = weight_grads(
+        rows, act, hidden, token_grad, scale, gate_weight.shape
+    )
+    return (hidden.reshape(hidden_grad.shape), grad_gate, grad_up, token_grad)
+
+
+def weight_grads(rows, act, hidden, token_grad, scale, shape):
     experts, model_width, hidden_units = shape
     chunks, _, width = rows.shape
     slots = act.shape[1]
     halves = 2
     count = chunks // halves
     out_block = pl.BlockSpec((1, count * width, hidden_units), lambda e, h: (e, h, 0))
+    token_block = pl.BlockSpec(token_grad.shape, lambda e, h: (0, 0))
     hidden_block = pl.BlockSpec((1, slots, hidden_units), lambda e, h: (e, 0, 0))
     return pl.pallas_call(
         functools.partial(weight_grad_kernel, count),
         grid=(experts, halves),
         out_shape=[jax.ShapeDtypeStruct(shape, BF16)] * 2
-        + [jax.ShapeDtypeStruct(hidden.shape, BF16)],
+        + [jax.ShapeDtypeStruct(hidden.shape, BF16), jax.ShapeDtypeStruct(token_grad.shape, BF16)],
         in_specs=[
             pl.BlockSpec((1, 1, 128), lambda e, h: (e, 0, 0)),
             pl.BlockSpec((count, slots, width), lambda e, h: (h, e, 0)),
             pl.BlockSpec((1, slots, 2 * hidden_units), lambda e, h: (e, 0, 0)),
             hidden_block,
+            token_block,
         ],
-        out_specs=[out_block, out_block, hidden_block],
+        out_specs=[out_block, out_block, hidden_block, token_block],
         cost_estimate=pl.CostEstimate(
             flops=4 * experts * slots * model_width * hidden_units,
             bytes_accessed=4 * experts * model_width * hidden_units + 2 * rows.size,
@@ -579,7 +585,7 @@
         ),
         compiler_params=pltpu.CompilerParams(vmem_limit_bytes=VMEM_LIMIT),
         name="weight_grads",
-    )(scale, rows, act, hidden)
+    )(scale, rows, act, hidden, token_grad)
 
 
 def solution(mesh):

time: 75.6 us -> 73.1 us (0.967)
  starting transfers between devices: 4.45 us -> 0 us
  Pallas kernels: 68.4 us -> 72.1 us
  other arithmetic: 1.59 us -> 0 us
    ppermute x3 -> x0, starting transfers between devices: 4.45 us -> none  [kernel_body(): arrived.append(lax.ppermute(totals[j], 'expert', pairs))]
    pallas_call x1, Pallas kernels: 54.2 us -> 57.7 us  [kernel_body(): pl.pallas_call(expert_kernel, out_shape=[jax.ShapeDtypeStruct((experts, s...]
    convert_element_type x1 -> x0, other arithmetic: 1.59 us -> none  [kernel_body(): token_grad.astype(BF16)]
  transfers between devices with their start and end apart: 3 -> 0, of which waited for: 0 -> 0; matrix products, arithmetic and copies ran while one was open for 0% -> 0% of each run, Pallas kernels for 19% -> 0%
where the time goes in v4:
time: 73.1 us; the launch traced here: 72.7 us
  Pallas kernels  72.1 us (99%)
    pallas_call x1, Pallas kernels, kernel_body(): pl.pallas_call(expert_kernel, out_shape=[jax.ShapeDtypeStruct((experts, s...  57.7 us
    pallas_call x1, Pallas kernels, weight_grads(): pl.pallas_call(functools.partial(weight_grad_kernel, count), grid=(expert...  14.3 us

profile of v4, /device:TPU:0, one launch (start us, length us, event | category | flops | bytes accessed | tf_op | source)
XLA Modules:
  0.0 72.7 jit_solution(16064624649443162264)
XLA Ops:
  0.6 57.7 %experts.1 = (bf16[4,128,512]{2,1,0:T(8,128)(2,1)}, bf16[4,128,1024]{2,1,0:T(8,128)(2,1)}, bf16[8,512,448]{2,1,0:T(8,128)(2,1)}, f32[4,1,128]{2,1,0:T(1,128)}, bf16[96,448]{1,0:T(8,128)(2,1)}) custom-call(bf16[96,448]{1,0:T(8,128)(2,1)} %tokens_ref.1, s32[8,384]{1,0:T(8,128)} %bitcast.4, bf16[4,128,512]{2,1,0:T(8,128)(2,1)} %bitcast.3, f32[4]{0:T(128)} %limit_ref.1, ...), custom_call_target="tpu_custom_call" | custom-call | tf_op jit(solution)/shard_map/experts/pallas_call | solution.py:517
  58.4 14.3 %weight_grads.1 = (bf16[4,3584,512]{2,1,0:T(8,128)(2,1)}, bf16[4,3584,512]{2,1,0:T(8,128)(2,1)}, bf16[4,128,512]{2,1,0:T(8,128)(2,1)}, bf16[96,448]{1,0:T(8,128)(2,1)}) custom-call(f32[4,1,128]{2,1,0:T(1,128)} %get-tuple-element.13.scale_ref, bf16[8,512,448]{2,1,0:T(8,128)(2,1)} %get-tuple-element.14.rows_ref, ...), custom_call_target="tpu_custom_call" | custom-call | flops 3758096384 | bytes 33030144 | tf_op jit(solution)/shard_map/weight_grads/pallas_call | solution.py:568
